TPU v7x, 32 devices: a whole 2x2x4 slice. The times are simulated.
32 devices in a mesh: ens: 2 (over y), gx: 4 (over z), gy: 2 (over x), lev: 2 (over core).
Axes of the slice: x: 2, y: 2, z: 4, core: 2. Of those that a mesh axis runs over, the one named last changes fastest.
Arguments:
- innovations: bfloat16 [8, 4, 256, 1024], P('ens', 'lev', 'gx', 'gy'), parts along dimension 0, may hold values from -18 to 18
- restrict_offsets: int32 [4, 2], P('lev'), may hold values from 0 to 3
- prolong_offsets: int32 [4, 2], P('lev'), may hold values from 0 to 3
- east_courant: float32 [8, 64, 256], P(('ens', 'lev'), 'gx', 'gy'), parts along dimension 0, may hold values from 0.05 to 0.45
- north_courant: float32 [8, 64, 256], P(('ens', 'lev'), 'gx', 'gy'), parts along dimension 0, may hold values from 0.05 to 0.45
- obs_weight: float32 [8, 64, 256], P(('ens', 'lev'), 'gx', 'gy'), parts along dimension 0, may hold values from 0.5 to 4
Outputs:
- increment_fine: float32 [8, 256, 1024], P(('ens', 'lev'), 'gx', 'gy'), parts along dimension 0
- residual_inner: float32 [8, 64, 256], P(('ens', 'lev'), 'gx', 'gy'), parts along dimension 0
There are 2 independent parts, one for each index of `ens`. A program takes and returns all parts, laid end to end along the dimension named above; an argument that names none is the same for every part. Nothing has to cross between parts.
All inputs are finite; a program needn't handle non-finite values.
Results may differ from a plain program's by a relative error of at most 0.0003.
Values may be sent and summed in bfloat16 or wider, within the bound.
A program may use at most 64 MiB of HBM per device.

v0:
```python
import jax
import jax.numpy as jnp
from jax import lax
from jax.sharding import PartitionSpec as P

ITERS = 2


tent_weights = (0.125, 0.375, 0.375, 0.125)


def from_behind(block, axis, distance):
    devices = range(lax.axis_size(axis))
    route = [(i - distance, i) for i in devices if i - distance in devices]
    return lax.ppermute(block, axis, route)


def extended_2(shard, sides, width):
    for axis, dim in sides:
        count, length = (lax.axis_size(axis), shard.shape[dim])
        up = [(i, (i + 1) % count) for i in range(count - 1)]
        down = [(j, i) for i, j in up]
        last = lax.slice_in_dim(shard, length - width, length, axis=dim)
        leading = lax.slice_in_dim(shard, 0, width, axis=dim)
        before = lax.ppermute(last, axis, up)
        after = lax.ppermute(leading, axis, down)
        shard = jnp.concatenate([before, shard, after], axis=dim)
    return shard


def restrict_matrix(offsets, coarse_len, ext_len):
    shape = (offsets.shape[0], coarse_len, ext_len)
    coarse_index = lax.broadcasted_iota(jnp.int32, shape, 1)
    ext_index = lax.broadcasted_iota(jnp.int32, shape, 2)
    tap_index = ext_index - 4 * coarse_index - offsets[:, None, None] - 1
    weights = jnp.zeros(shape, jnp.float32)
    for position in range(4):
        weights = weights + jnp.where(tap_index == position, tent_weights[position], 0.0)
    return weights


def prolong_matrix(offsets, fine_len, ext_len):
    shape = (offsets.shape[0], fine_len, ext_len)
    fine_index = lax.broadcasted_iota(jnp.int32, shape, 1)
    ext_index = lax.broadcasted_iota(jnp.int32, shape, 2)
    shifted = fine_index - offsets[:, None, None]
    lower = jnp.floor_divide(shifted, 4)
    upper_weight = (shifted - 4 * lower).astype(jnp.float32) * 0.25
    return jnp.where(ext_index == lower + 1, 1.0 - upper_weight, 0.0) + jnp.where(
        ext_index == lower + 2, upper_weight, 0.0
    )


def edges_lon(values, offset_by):
    return from_behind(values, "gx", offset_by)


def edges_lat(values, offset_by):
    return from_behind(values, "gy", offset_by)


def lower_ext(values, depth):
    west = edges_lon(values[..., -depth:, :], 1)
    middle = jnp.concatenate([west, values], axis=-2)
    source = jnp.concatenate([jnp.zeros_like(west), values], axis=-2)
    south = edges_lat(source[..., -depth:], 1)
    return jnp.concatenate([south, middle], axis=-1)


def tangent_ext(state, east_c, north_c):
    west = jnp.concatenate([jnp.zeros_like(state[..., :1, :]), state[..., :-1, :]], axis=-2)
    south = jnp.concatenate([jnp.zeros_like(state[..., :1]), state[..., :-1]], axis=-1)
    return (1.0 - east_c - north_c) * state + east_c * west + north_c * south


def adjoint_step(state, east_c, north_c):
    east_part = east_c * state
    north_part = north_c * state
    east_rim = edges_lon(east_part[..., :1, :], -1)
    north_rim = edges_lat(north_part[..., :1], -1)
    east_full = jnp.concatenate([east_part[..., 1:, :], east_rim], axis=-2)
    north_full = jnp.concatenate([north_part[..., 1:], north_rim], axis=-1)
    return (1.0 - east_c - north_c) * state + east_full + north_full


def grand_total(values):
    return lax.psum((values[0],), ("gx", "gy", "lev"))


def on_device(
    innovations, restrict_offsets, prolong_offsets, east_courant, north_courant, obs_weight
):
    steps_count, levels, fine_x, fine_y = innovations.shape
    coarse_x = fine_x // 4
    coarse_y = fine_y // 4
    extended = extended_2(innovations, (("gx", 2), ("gy", 3)), 2)
    row_weights = restrict_matrix(restrict_offsets[:, 0], coarse_x, fine_x + 4).astype(jnp.bfloat16)
    col_weights = restrict_matrix(restrict_offsets[:, 1], coarse_y, fine_y + 4)
    partial_rows = jnp.einsum(
        "lce,tlem->tlcm", row_weights, extended, preferred_element_type=jnp.float32
    )
    restricted = jnp.einsum(
        "tlcm,ldm->tlcd",
        partial_rows,
        col_weights,
        precision=lax.Precision.HIGHEST,
        preferred_element_type=jnp.float32,
    )
    courant = jnp.stack([east_courant, north_courant])
    east_c = courant[0]
    north_c = courant[1]
    ext_courant = jnp.pad(courant, ((0, 0), (0, 0), (1, 0), (1, 0)))
    adjoint_state = obs_weight * restricted[steps_count - 1]
    for time_index in range(steps_count - 2, -1, -1):
        adjoint_state = (
            adjoint_step(adjoint_state, east_c, north_c) + obs_weight * restricted[time_index]
        )
    gradient_rhs = adjoint_step(adjoint_state, east_c, north_c)
    solution = jnp.zeros_like(gradient_rhs)
    residual = gradient_rhs
    direction = gradient_rhs
    norm_now = grand_total((jnp.sum(residual * residual),))[0]
    for iteration in range(ITERS):
        states = []
        state = direction
        for hessian_time_index in range(steps_count):
            ext_state = lower_ext(state, 1)
            state = tangent_ext(ext_state, ext_courant[0], ext_courant[1])[..., 1:, 1:]
            states.append(state)
        lam = obs_weight * states[steps_count - 1]
        for hessian_time_index in range(steps_count - 2, -1, -1):
            lam = adjoint_step(lam, east_c, north_c) + obs_weight * states[hessian_time_index]
        image = direction + adjoint_step(lam, east_c, north_c)
        states, image = (states, image)
        curvature = grand_total((jnp.sum(direction * image),))[0]
        alpha = norm_now / curvature
        solution = solution + alpha * direction
        residual = residual - alpha * image
        if iteration + 1 < ITERS:
            norm_next = grand_total((jnp.sum(residual * residual),))[0]
            direction = residual + norm_next / norm_now * direction
            norm_now = norm_next
    coarse_ext = extended_2(solution, (("gx", 1), ("gy", 2)), 1)
    rows_prolong = prolong_matrix(prolong_offsets[:, 0], fine_x, coarse_x + 2)
    cols_prolong = prolong_matrix(prolong_offsets[:, 1], fine_y, coarse_y + 2)
    half_done = jnp.einsum(
        "lfk,lkm->lfm",
        rows_prolong,
        coarse_ext,
        precision=lax.Precision.HIGHEST,
        preferred_element_type=jnp.float32,
    )
    increment = jnp.einsum(
        "lfm,lgm->lfg",
        half_done,
        cols_prolong,
        precision=lax.Precision.HIGHEST,
        preferred_element_type=jnp.float32,
    )
    return (increment, residual)


def solution(mesh):
    in_specs = (
        P("ens", "lev", "gx", "gy"),
        P("lev", None),
        P("lev", None),
        P(("ens", "lev"), "gx", "gy"),
        P(("ens", "lev"), "gx", "gy"),
        P(("ens", "lev"), "gx", "gy"),
    )
    out_specs = (P(("ens", "lev"), "gx", "gy"), P(("ens", "lev"), "gx", "gy"))
    return jax.shard_map(
        on_device, mesh=mesh, in_specs=in_specs, out_specs=out_specs, check_vma=False
    )
```

profile of v0, /device:TPU:0, one launch (start us, length us, event | category | flops | bytes accessed | tf_op | source)
XLA Modules:
  0.0 293.9 jit_solution(9083238990340562762)
XLA Ops:
  1.6 4.9 %collective-permute-start = (bf16[4,2,2,512]{3,2,1,0:T(2,128)(2,1)S(1)}, bf16[4,2,2,512]{3,2,1,0:T(2,128)(2,1)S(1)}, u32[]{:S(2)}, u32[]{:S(2)}) collective-permute-start(bf16[4,2,2,512]{3,2,1,0:T(2,128)(2,1)S(1)} %get-tuple-element.38), channel_id=1, source_target_pairs={{0,4},{4,8},{8,12},{1,5},{5,9},{9,13},{2,6},{6,10},{10,14},{3,7},{... | collective-permute-start | bytes 49160 | tf_op jit(solution)/shard_map/ppermute | solution.py:25
  19.3 4.4 %collective-permute-done.3 = bf16[4,2,68,2]{3,2,1,0:T(8,128)(2,1)S(1)} collective-permute-done((bf16[4,2,68,2]{3,2,1,0:T(8,128)(2,1)S(1)}, bf16[4,2,68,2]{3,2,1,0:T(8,128)(2,1)S(1)}, u32[]{:S(2)}, u32[]{:S(2)}) %collective-permute-start.3) | collective-permute-done | bytes 2208 | tf_op jit(solution)/shard_map/ppermute | solution.py:26
  28.0 4.2 %collective-permute-done.5 = f32[2,16,1]{2,1,0:T(8,128)S(1)} collective-permute-done((f32[2,16,1]{2,1,0:T(8,128)S(1)}, f32[2,16,1]{2,1,0:T(8,128)S(1)}, u32[]{:S(2)}, u32[]{:S(2)}) %collective-permute-start.5) | collective-permute-done | bytes 160 | tf_op jit(solution)/shard_map/ppermute | solution.py:15
  35.0 4.2 %collective-permute-done.7 = f32[2,16,1]{2,1,0:T(8,128)S(1)} collective-permute-done((f32[2,16,1]{2,1,0:T(8,128)S(1)}, f32[2,16,1]{2,1,0:T(8,128)S(1)}, u32[]{:S(2)}, u32[]{:S(2)}) %collective-permute-start.7) | collective-permute-done | bytes 160 | tf_op jit(solution)/shard_map/ppermute | solution.py:15
  42.0 4.2 %collective-permute-done.9 = f32[2,16,1]{2,1,0:T(8,128)S(1)} collective-permute-done((f32[2,16,1]{2,1,0:T(8,128)S(1)}, f32[2,16,1]{2,1,0:T(8,128)S(1)}, u32[]{:S(2)}, u32[]{:S(2)}) %collective-permute-start.9) | collective-permute-done | bytes 160 | tf_op jit(solution)/shard_map/ppermute | solution.py:15
  49.1 4.2 %collective-permute-done.11 = f32[2,16,1]{2,1,0:T(8,128)S(1)} collective-permute-done((f32[2,16,1]{2,1,0:T(8,128)S(1)}, f32[2,16,1]{2,1,0:T(8,128)S(1)}, u32[]{:S(2)}, u32[]{:S(2)}) %collective-permute-start.11) | collective-permute-done | bytes 160 | tf_op jit(solution)/shard_map/ppermute | solution.py:15
  55.5 6.1 %collective-permute-start.13 = (f32[2,1,128]{2,1,0:T(1,128)S(1)}, f32[2,1,128]{2,1,0:T(1,128)S(1)}, u32[]{:S(2)}, u32[]{:S(2)}) collective-permute-start(f32[2,1,128]{2,1,0:T(1,128)S(1)} %slice.466), channel_id=1, source_target_pairs={{0,4},{4,8},{8,12},{1,5},{5,9},{9,13},{2,6},{6,10},{10,14},{3,7},{... | collective-permute-start | bytes 3080 | tf_op jit(solution)/shard_map/ppermute | solution.py:15
  74.7 4.2 %collective-permute-start.16 = (f32[2,17,1]{2,1,0:T(8,128)S(1)}, f32[2,17,1]{2,1,0:T(8,128)S(1)}, u32[]{:S(2)}, u32[]{:S(2)}) collective-permute-start(f32[2,17,1]{2,1,0:T(8,128)S(1)} %pad_slice_fusion.5), channel_id=1, source_target_pairs={{0,2},{1,3},{4,6},{5,7},{8,10},{9,11},{12,14},{13,15},{16,18},{17,... | collective-permute-start | bytes 416 | tf_op jit(solution)/shard_map/ppermute | solution.py:15
  80.9 4.2 %collective-permute-start.18 = (f32[2,17,1]{2,1,0:T(8,128)S(1)}, f32[2,17,1]{2,1,0:T(8,128)S(1)}, u32[]{:S(2)}, u32[]{:S(2)}) collective-permute-start(f32[2,17,1]{2,1,0:T(8,128)S(1)} %pad_slice_fusion.4), channel_id=1, source_target_pairs={{0,2},{1,3},{4,6},{5,7},{8,10},{9,11},{12,14},{13,15},{16,18},{17,... | collective-permute-start | bytes 416 | tf_op jit(solution)/shard_map/ppermute | solution.py:15
  93.1 4.2 %collective-permute-done.21 = f32[2,16,1]{2,1,0:T(8,128)S(1)} collective-permute-done((f32[2,16,1]{2,1,0:T(8,128)S(1)}, f32[2,16,1]{2,1,0:T(8,128)S(1)}, u32[]{:S(2)}, u32[]{:S(2)}) %collective-permute-start.21) | collective-permute-done | bytes 160 | tf_op jit(solution)/shard_map/ppermute | solution.py:15
  100.2 4.2 %collective-permute-done.23 = f32[2,16,1]{2,1,0:T(8,128)S(1)} collective-permute-done((f32[2,16,1]{2,1,0:T(8,128)S(1)}, f32[2,16,1]{2,1,0:T(8,128)S(1)}, u32[]{:S(2)}, u32[]{:S(2)}) %collective-permute-start.23) | collective-permute-done | bytes 160 | tf_op jit(solution)/shard_map/ppermute | solution.py:15
  107.2 4.2 %collective-permute-done.25 = f32[2,16,1]{2,1,0:T(8,128)S(1)} collective-permute-done((f32[2,16,1]{2,1,0:T(8,128)S(1)}, f32[2,16,1]{2,1,0:T(8,128)S(1)}, u32[]{:S(2)}, u32[]{:S(2)}) %collective-permute-start.25) | collective-permute-done | bytes 160 | tf_op jit(solution)/shard_map/ppermute | solution.py:15
  114.3 4.2 %collective-permute-done.27 = f32[2,16,1]{2,1,0:T(8,128)S(1)} collective-permute-done((f32[2,16,1]{2,1,0:T(8,128)S(1)}, f32[2,16,1]{2,1,0:T(8,128)S(1)}, u32[]{:S(2)}, u32[]{:S(2)}) %collective-permute-start.27) | collective-permute-done | bytes 160 | tf_op jit(solution)/shard_map/ppermute | solution.py:15
  119.9 31.5 %all-reduce.25 = (f32[]{:T(128)}, f32[]{:T(128)}) all-reduce(f32[]{:T(128)} %get-tuple-element.3, f32[]{:T(128)} %get-tuple-element.2), channel_id=1, replica_groups=mesh['ens'=2,'gx'=4,'gy'=2,'lev'=2] {'gx','gy','lev'}, use_global_device_ids=true, to_apply=%region_1.2 | all-reduce | flops 2 | bytes 16 | tf_op jit(solution)/shard_map/psum | solution.py:87
  153.3 30.4 %psum.30 = f32[]{:T(128)} all-reduce(f32[]{:T(128)} %multiply_reduce_fusion.1), channel_id=1, replica_groups=mesh['ens'=2,'gx'=4,'gy'=2,'lev'=2] {'gx','gy','lev'}, use_global_device_ids=true, to_apply=%region_5.6 | all-reduce | flops 1 | bytes 8 | tf_op jit(solution)/shard_map/psum | solution.py:87
  197.1 4.4 %collective-permute-start.33 = (f32[2,1,128]{2,1,0:T(1,128)S(1)}, f32[2,1,128]{2,1,0:T(1,128)S(1)}, u32[]{:S(2)}, u32[]{:S(2)}) collective-permute-start(f32[2,1,128]{2,1,0:T(1,128)S(1)} %slice.509), channel_id=1, source_target_pairs={{0,4},{4,8},{8,12},{1,5},{5,9},{9,13},{2,6},{6,10},{10,14},{3,7},{... | collective-permute-start | bytes 3080 | tf_op jit(solution)/shard_map/ppermute | solution.py:15
  201.5 4.2 %collective-permute-start.32 = (f32[2,17,1]{2,1,0:T(8,128)S(1)}, f32[2,17,1]{2,1,0:T(8,128)S(1)}, u32[]{:S(2)}, u32[]{:S(2)}) collective-permute-start(f32[2,17,1]{2,1,0:T(8,128)S(1)} %pad_slice_fusion.1), channel_id=1, source_target_pairs={{0,2},{1,3},{4,6},{5,7},{8,10},{9,11},{12,14},{13,15},{16,18},{17,... | collective-permute-start | bytes 416 | tf_op jit(solution)/shard_map/ppermute | solution.py:15
  209.6 4.2 %collective-permute-start.34 = (f32[2,17,1]{2,1,0:T(8,128)S(1)}, f32[2,17,1]{2,1,0:T(8,128)S(1)}, u32[]{:S(2)}, u32[]{:S(2)}) collective-permute-start(f32[2,17,1]{2,1,0:T(8,128)S(1)} %pad_slice_fusion), channel_id=1, source_target_pairs={{0,2},{1,3},{4,6},{5,7},{8,10},{9,11},{12,14},{13,15},{16,18},{17,... | collective-permute-start | bytes 416 | tf_op jit(solution)/shard_map/ppermute | solution.py:15
  218.3 4.2 %collective-permute-done.37 = f32[2,16,1]{2,1,0:T(8,128)S(1)} collective-permute-done((f32[2,16,1]{2,1,0:T(8,128)S(1)}, f32[2,16,1]{2,1,0:T(8,128)S(1)}, u32[]{:S(2)}, u32[]{:S(2)}) %collective-permute-start.37) | collective-permute-done | bytes 160 | tf_op jit(solution)/shard_map/ppermute | solution.py:15
  225.3 4.2 %collective-permute-done.39 = f32[2,16,1]{2,1,0:T(8,128)S(1)} collective-permute-done((f32[2,16,1]{2,1,0:T(8,128)S(1)}, f32[2,16,1]{2,1,0:T(8,128)S(1)}, u32[]{:S(2)}, u32[]{:S(2)}) %collective-permute-start.39) | collective-permute-done | bytes 160 | tf_op jit(solution)/shard_map/ppermute | solution.py:15
  232.4 4.2 %collective-permute-done.41 = f32[2,16,1]{2,1,0:T(8,128)S(1)} collective-permute-done((f32[2,16,1]{2,1,0:T(8,128)S(1)}, f32[2,16,1]{2,1,0:T(8,128)S(1)}, u32[]{:S(2)}, u32[]{:S(2)}) %collective-permute-start.41) | collective-permute-done | bytes 160 | tf_op jit(solution)/shard_map/ppermute | solution.py:15
  239.4 4.2 %collective-permute-done.43 = f32[2,16,1]{2,1,0:T(8,128)S(1)} collective-permute-done((f32[2,16,1]{2,1,0:T(8,128)S(1)}, f32[2,16,1]{2,1,0:T(8,128)S(1)}, u32[]{:S(2)}, u32[]{:S(2)}) %collective-permute-start.43) | collective-permute-done | bytes 160 | tf_op jit(solution)/shard_map/ppermute | solution.py:15
  244.8 31.5 %psum.31 = f32[]{:T(128)} all-reduce(f32[]{:T(128)} %get-tuple-element.10), channel_id=1, replica_groups=mesh['ens'=2,'gx'=4,'gy'=2,'lev'=2] {'gx','gy','lev'}, use_global_device_ids=true, to_apply=%region_7.8 | all-reduce | flops 1 | bytes 8 | tf_op jit(solution)/shard_map/psum | solution.py:87
  287.9 4.2 %collective-permute-done.47 = f32[2,18,1]{2,1,0:T(8,128)S(1)} collective-permute-done((f32[2,18,1]{2,1,0:T(8,128)S(1)}, f32[2,18,1]{2,1,0:T(8,128)S(1)}, u32[]{:S(2)}, u32[]{:S(2)}) %collective-permute-start.47) | collective-permute-done | bytes 176 | tf_op jit(solution)/shard_map/ppermute | solution.py:26
  (217 shorter events, 102.9 us)
Async XLA Ops:
  1.6 7.2 %collective-permute-start = (bf16[4,2,2,512]{3,2,1,0:T(2,128)(2,1)S(1)}, bf16[4,2,2,512]{3,2,1,0:T(2,128)(2,1)S(1)}, u32[]{:S(2)}, u32[]{:S(2)}) collective-permute-start(bf16[4,2,2,512]{3,2,1,0:T(2,128)(2,1)S(1)} %get-tuple-element.38), channel_id=1, source_target_pairs={{0,4},{4,8},{8,12},{1,5},{5,9},{9,13},{2,6},{6,10},{10,14},{3,7},{... | collective-permute-start | bytes 49160 | tf_op jit(solution)/shard_map/ppermute | solution.py:25
  13.3 6.1 %collective-permute-start.2 = (bf16[4,2,68,2]{3,2,1,0:T(8,128)(2,1)S(1)}, bf16[4,2,68,2]{3,2,1,0:T(8,128)(2,1)S(1)}, u32[]{:S(2)}, u32[]{:S(2)}) collective-permute-start(bf16[4,2,68,2]{3,2,1,0:T(8,128)(2,1)S(1)} %get-tuple-element.36), channel_id=1, source_target_pairs={{0,2},{1,3},{4,6},{5,7},{8,10},{9,11},{12,14},{13,15},{16,18},{17,... | collective-permute-start | bytes 6536 | tf_op jit(solution)/shard_map/ppermute | solution.py:25
  16.7 7.0 %collective-permute-start.3 = (bf16[4,2,68,2]{3,2,1,0:T(8,128)(2,1)S(1)}, bf16[4,2,68,2]{3,2,1,0:T(8,128)(2,1)S(1)}, u32[]{:S(2)}, u32[]{:S(2)}) collective-permute-start(bf16[4,2,68,2]{3,2,1,0:T(8,128)(2,1)S(1)} %get-tuple-element.37), channel_id=1, source_target_pairs={{2,0},{3,1},{6,4},{7,5},{10,8},{11,9},{14,12},{15,13},{18,16},{19,... | collective-permute-start | bytes 6536 | tf_op jit(solution)/shard_map/ppermute | solution.py:26
  25.3 6.9 %collective-permute-start.4 = (f32[2,1,128]{2,1,0:T(1,128)S(1)}, f32[2,1,128]{2,1,0:T(1,128)S(1)}, u32[]{:S(2)}, u32[]{:S(2)}) collective-permute-start(f32[2,1,128]{2,1,0:T(1,128)S(1)} %slice.446), channel_id=1, source_target_pairs={{4,0},{8,4},{12,8},{5,1},{9,5},{13,9},{6,2},{10,6},{14,10},{7,3},{... | collective-permute-start | bytes 3080 | tf_op jit(solution)/shard_map/ppermute | solution.py:15
  32.3 6.9 %collective-permute-start.6 = (f32[2,1,128]{2,1,0:T(1,128)S(1)}, f32[2,1,128]{2,1,0:T(1,128)S(1)}, u32[]{:S(2)}, u32[]{:S(2)}) collective-permute-start(f32[2,1,128]{2,1,0:T(1,128)S(1)} %slice.451), channel_id=1, source_target_pairs={{4,0},{8,4},{12,8},{5,1},{9,5},{13,9},{6,2},{10,6},{14,10},{7,3},{... | collective-permute-start | bytes 3080 | tf_op jit(solution)/shard_map/ppermute | solution.py:15
  39.4 6.9 %collective-permute-start.8 = (f32[2,1,128]{2,1,0:T(1,128)S(1)}, f32[2,1,128]{2,1,0:T(1,128)S(1)}, u32[]{:S(2)}, u32[]{:S(2)}) collective-permute-start(f32[2,1,128]{2,1,0:T(1,128)S(1)} %slice.456), channel_id=1, source_target_pairs={{4,0},{8,4},{12,8},{5,1},{9,5},{13,9},{6,2},{10,6},{14,10},{7,3},{... | collective-permute-start | bytes 3080 | tf_op jit(solution)/shard_map/ppermute | solution.py:15
  46.4 7.5 %collective-permute-start.10 = (f32[2,1,128]{2,1,0:T(1,128)S(1)}, f32[2,1,128]{2,1,0:T(1,128)S(1)}, u32[]{:S(2)}, u32[]{:S(2)}) collective-permute-start(f32[2,1,128]{2,1,0:T(1,128)S(1)} %slice.461), channel_id=1, source_target_pairs={{4,0},{8,4},{12,8},{5,1},{9,5},{13,9},{6,2},{10,6},{14,10},{7,3},{... | collective-permute-start | bytes 3080 | tf_op jit(solution)/shard_map/ppermute | solution.py:15
  54.0 7.8 %collective-permute-start.12 = (f32[2,17,1]{2,1,0:T(8,128)S(1)}, f32[2,17,1]{2,1,0:T(8,128)S(1)}, u32[]{:S(2)}, u32[]{:S(2)}) collective-permute-start(f32[2,17,1]{2,1,0:T(8,128)S(1)} %pad_slice_fusion.7), channel_id=1, source_target_pairs={{0,2},{1,3},{4,6},{5,7},{8,10},{9,11},{12,14},{13,15},{16,18},{17,... | collective-permute-start | bytes 416 | tf_op jit(solution)/shard_map/ppermute | solution.py:15
  55.5 7.4 %collective-permute-start.13 = (f32[2,1,128]{2,1,0:T(1,128)S(1)}, f32[2,1,128]{2,1,0:T(1,128)S(1)}, u32[]{:S(2)}, u32[]{:S(2)}) collective-permute-start(f32[2,1,128]{2,1,0:T(1,128)S(1)} %slice.466), channel_id=1, source_target_pairs={{0,4},{4,8},{8,12},{1,5},{5,9},{9,13},{2,6},{6,10},{10,14},{3,7},{... | collective-permute-start | bytes 3080 | tf_op jit(solution)/shard_map/ppermute | solution.py:15
  63.3 7.0 %collective-permute-start.15 = (f32[2,1,128]{2,1,0:T(1,128)S(1)}, f32[2,1,128]{2,1,0:T(1,128)S(1)}, u32[]{:S(2)}, u32[]{:S(2)}) collective-permute-start(f32[2,1,128]{2,1,0:T(1,128)S(1)} %slice.470), channel_id=1, source_target_pairs={{0,4},{4,8},{8,12},{1,5},{5,9},{9,13},{2,6},{6,10},{10,14},{3,7},{... | collective-permute-start | bytes 3080 | tf_op jit(solution)/shard_map/ppermute | solution.py:15
  70.7 9.7 %collective-permute-start.17 = (f32[2,1,128]{2,1,0:T(1,128)S(1)}, f32[2,1,128]{2,1,0:T(1,128)S(1)}, u32[]{:S(2)}, u32[]{:S(2)}) collective-permute-start(f32[2,1,128]{2,1,0:T(1,128)S(1)} %slice.474), channel_id=1, source_target_pairs={{0,4},{4,8},{8,12},{1,5},{5,9},{9,13},{2,6},{6,10},{10,14},{3,7},{... | collective-permute-start | bytes 3080 | tf_op jit(solution)/shard_map/ppermute | solution.py:15
  80.9 8.0 %collective-permute-start.18 = (f32[2,17,1]{2,1,0:T(8,128)S(1)}, f32[2,17,1]{2,1,0:T(8,128)S(1)}, u32[]{:S(2)}, u32[]{:S(2)}) collective-permute-start(f32[2,17,1]{2,1,0:T(8,128)S(1)} %pad_slice_fusion.4), channel_id=1, source_target_pairs={{0,2},{1,3},{4,6},{5,7},{8,10},{9,11},{12,14},{13,15},{16,18},{17,... | collective-permute-start | bytes 416 | tf_op jit(solution)/shard_map/ppermute | solution.py:15
  90.4 6.9 %collective-permute-start.20 = (f32[2,1,128]{2,1,0:T(1,128)S(1)}, f32[2,1,128]{2,1,0:T(1,128)S(1)}, u32[]{:S(2)}, u32[]{:S(2)}) collective-permute-start(f32[2,1,128]{2,1,0:T(1,128)S(1)} %slice.486), channel_id=1, source_target_pairs={{4,0},{8,4},{12,8},{5,1},{9,5},{13,9},{6,2},{10,6},{14,10},{7,3},{... | collective-permute-start | bytes 3080 | tf_op jit(solution)/shard_map/ppermute | solution.py:15
  97.5 6.9 %collective-permute-start.22 = (f32[2,1,128]{2,1,0:T(1,128)S(1)}, f32[2,1,128]{2,1,0:T(1,128)S(1)}, u32[]{:S(2)}, u32[]{:S(2)}) collective-permute-start(f32[2,1,128]{2,1,0:T(1,128)S(1)} %slice.490), channel_id=1, source_target_pairs={{4,0},{8,4},{12,8},{5,1},{9,5},{13,9},{6,2},{10,6},{14,10},{7,3},{... | collective-permute-start | bytes 3080 | tf_op jit(solution)/shard_map/ppermute | solution.py:15
  104.5 7.0 %collective-permute-start.24 = (f32[2,1,128]{2,1,0:T(1,128)S(1)}, f32[2,1,128]{2,1,0:T(1,128)S(1)}, u32[]{:S(2)}, u32[]{:S(2)}) collective-permute-start(f32[2,1,128]{2,1,0:T(1,128)S(1)} %slice.494), channel_id=1, source_target_pairs={{4,0},{8,4},{12,8},{5,1},{9,5},{13,9},{6,2},{10,6},{14,10},{7,3},{... | collective-permute-start | bytes 3080 | tf_op jit(solution)/shard_map/ppermute | solution.py:15
  111.6 7.6 %collective-permute-start.26 = (f32[2,1,128]{2,1,0:T(1,128)S(1)}, f32[2,1,128]{2,1,0:T(1,128)S(1)}, u32[]{:S(2)}, u32[]{:S(2)}) collective-permute-start(f32[2,1,128]{2,1,0:T(1,128)S(1)} %slice.498), channel_id=1, source_target_pairs={{4,0},{8,4},{12,8},{5,1},{9,5},{13,9},{6,2},{10,6},{14,10},{7,3},{... | collective-permute-start | bytes 3080 | tf_op jit(solution)/shard_map/ppermute | solution.py:15
  189.6 7.1 %collective-permute-start.31 = (f32[2,1,128]{2,1,0:T(1,128)S(1)}, f32[2,1,128]{2,1,0:T(1,128)S(1)}, u32[]{:S(2)}, u32[]{:S(2)}) collective-permute-start(f32[2,1,128]{2,1,0:T(1,128)S(1)} %slice.505), channel_id=1, source_target_pairs={{0,4},{4,8},{8,12},{1,5},{5,9},{9,13},{2,6},{6,10},{10,14},{3,7},{... | collective-permute-start | bytes 3080 | tf_op jit(solution)/shard_map/ppermute | solution.py:15
  197.1 10.2 %collective-permute-start.33 = (f32[2,1,128]{2,1,0:T(1,128)S(1)}, f32[2,1,128]{2,1,0:T(1,128)S(1)}, u32[]{:S(2)}, u32[]{:S(2)}) collective-permute-start(f32[2,1,128]{2,1,0:T(1,128)S(1)} %slice.509), channel_id=1, source_target_pairs={{0,4},{4,8},{8,12},{1,5},{5,9},{9,13},{2,6},{6,10},{10,14},{3,7},{... | collective-permute-start | bytes 3080 | tf_op jit(solution)/shard_map/ppermute | solution.py:15
  207.6 7.7 %collective-permute-start.35 = (f32[2,1,128]{2,1,0:T(1,128)S(1)}, f32[2,1,128]{2,1,0:T(1,128)S(1)}, u32[]{:S(2)}, u32[]{:S(2)}) collective-permute-start(f32[2,1,128]{2,1,0:T(1,128)S(1)} %slice.513), channel_id=1, source_target_pairs={{0,4},{4,8},{8,12},{1,5},{5,9},{9,13},{2,6},{6,10},{10,14},{3,7},{... | collective-permute-start | bytes 3080 | tf_op jit(solution)/shard_map/ppermute | solution.py:15
  215.6 6.9 %collective-permute-start.36 = (f32[2,1,128]{2,1,0:T(1,128)S(1)}, f32[2,1,128]{2,1,0:T(1,128)S(1)}, u32[]{:S(2)}, u32[]{:S(2)}) collective-permute-start(f32[2,1,128]{2,1,0:T(1,128)S(1)} %slice.521), channel_id=1, source_target_pairs={{4,0},{8,4},{12,8},{5,1},{9,5},{13,9},{6,2},{10,6},{14,10},{7,3},{... | collective-permute-start | bytes 3080 | tf_op jit(solution)/shard_map/ppermute | solution.py:15
  222.6 6.9 %collective-permute-start.38 = (f32[2,1,128]{2,1,0:T(1,128)S(1)}, f32[2,1,128]{2,1,0:T(1,128)S(1)}, u32[]{:S(2)}, u32[]{:S(2)}) collective-permute-start(f32[2,1,128]{2,1,0:T(1,128)S(1)} %slice.525), channel_id=1, source_target_pairs={{4,0},{8,4},{12,8},{5,1},{9,5},{13,9},{6,2},{10,6},{14,10},{7,3},{... | collective-permute-start | bytes 3080 | tf_op jit(solution)/shard_map/ppermute | solution.py:15
  229.7 6.9 %collective-permute-start.40 = (f32[2,1,128]{2,1,0:T(1,128)S(1)}, f32[2,1,128]{2,1,0:T(1,128)S(1)}, u32[]{:S(2)}, u32[]{:S(2)}) collective-permute-start(f32[2,1,128]{2,1,0:T(1,128)S(1)} %slice.529), channel_id=1, source_target_pairs={{4,0},{8,4},{12,8},{5,1},{9,5},{13,9},{6,2},{10,6},{14,10},{7,3},{... | collective-permute-start | bytes 3080 | tf_op jit(solution)/shard_map/ppermute | solution.py:15
  236.7 7.4 %collective-permute-start.42 = (f32[2,1,128]{2,1,0:T(1,128)S(1)}, f32[2,1,128]{2,1,0:T(1,128)S(1)}, u32[]{:S(2)}, u32[]{:S(2)}) collective-permute-start(f32[2,1,128]{2,1,0:T(1,128)S(1)} %slice.533), channel_id=1, source_target_pairs={{4,0},{8,4},{12,8},{5,1},{9,5},{13,9},{6,2},{10,6},{14,10},{7,3},{... | collective-permute-start | bytes 3080 | tf_op jit(solution)/shard_map/ppermute | solution.py:15
  286.4 5.7 %collective-permute-start.47 = (f32[2,18,1]{2,1,0:T(8,128)S(1)}, f32[2,18,1]{2,1,0:T(8,128)S(1)}, u32[]{:S(2)}, u32[]{:S(2)}) collective-permute-start(f32[2,18,1]{2,1,0:T(8,128)S(1)} %get-tuple-element.47), channel_id=1, source_target_pairs={{2,0},{3,1},{6,4},{7,5},{10,8},{11,9},{14,12},{15,13},{18,16},{19,... | collective-permute-start | bytes 440 | tf_op jit(solution)/shard_map/ppermute | solution.py:26
  (29 other events, 211.3 us)
where the time goes:
time: 295 us; the launch traced here: 294 us
  starting transfers between devices  99.1 us (34%)
  blocking collectives  93.4 us (32%)
  waiting for transfers between devices  81.6 us (28%)
  other arithmetic  6.11 us (2%)
  between operations  5.74 us (2%)
  local copies, waits for them, and re-layouts  4.73 us (2%)
  matrix products  3.24 us (1%)
    psum x3, blocking collectives, grand_total(): return lax.psum((values[0],), ('gx', 'gy', 'lev'))  93.4 us
    ppermute x40, starting transfers between devices, from_behind(): return lax.ppermute(block, axis, route)  83 us
    ppermute x40, waiting for transfers between devices, from_behind(): return lax.ppermute(block, axis, route)  64.1 us
    ppermute x4, waiting for transfers between devices, extended_2(): after = lax.ppermute(leading, axis, down)  16.1 us
    ppermute x4, starting transfers between devices, extended_2(): before = lax.ppermute(last, axis, up)  10.9 us
  transfers between devices with their start and end apart: 48, of which 28 were waited for; matrix products, arithmetic and copies ran while one was open for 1% of the time, Pallas kernels for 0%

commit v1 on v0

v1 whole, which is shorter than its diff:
```python
import functools

import jax
import jax.numpy as jnp
from jax import lax
from jax.experimental import pallas as pl
from jax.experimental.pallas import tpu as pltpu
from jax.sharding import PartitionSpec as P

MESH = pl.DeviceIdType.MESH
HALO = 8
F32, BF16 = jnp.float32, jnp.bfloat16


def repeat(count, body):
    if count <= 16:
        for k in range(1, count):
            body(k)
    else:
        lax.fori_loop(1, count, lambda k, carry: (body(k), carry)[1], 0)


def split(values):
    high = values.astype(BF16)
    return high, (values - high.astype(F32)).astype(BF16)


def dot(a, b):
    return jnp.dot(a, b, preferred_element_type=F32)


def split_dot(values, weights):
    high, low = split(values)
    return dot(high, weights) + dot(low, weights)


def iota(shape, dim):
    return lax.broadcasted_iota(jnp.int32, shape, dim)


def kernel(
    sizes, inn, r_off, p_off, east, north, weight, out, res, coef, gx_in, gy_in, gx_out, gy_out,
    red, c_send, c_recv, g_send, g_recv, r_send, r_recv,
):
    nx, ny, nl = sizes
    group = nx * ny * nl
    steps, levels, fine_x, fine_y = inn.shape
    rows, cols = fine_x // 4, fine_y // 4
    ext = rows + 2 * HALO
    wide = 2 * cols
    ix, iy, il = lax.axis_index("gx"), lax.axis_index("gy"), lax.axis_index("lev")
    me = (ix * ny + iy) * nl + il

    def peer(k):
        other = lax.rem(me + k, group)
        return {
            "gx": other // (ny * nl),
            "gy": lax.rem(other // nl, ny),
            "lev": lax.rem(other, nl),
        }

    coef[...] = jnp.zeros_like(coef)
    gx_in[...] = jnp.zeros_like(gx_in)
    gy_in[...] = jnp.zeros_like(gy_in)
    for field, ref in enumerate((east, north, weight)):
        coef[0, field, :, HALO : HALO + rows, :] = ref[...]
    barrier = pltpu.get_barrier_semaphore()
    repeat(group, lambda k: pl.semaphore_signal(barrier, inc=1, device_id=peer(k), device_id_type=MESH))
    pl.semaphore_wait(barrier, group - 1)

    sides = [(dx, dy) for dx in (0, 1, -1) for dy in (0, 1, -1) if (dx, dy) != (0, 0)]
    sides = [(dx, dy) for dx, dy in sides if (nx > 1 or not dx) and (ny > 1 or not dy)]

    def present(dx, dy):
        x, y = ix + dx, iy + dy
        return (x >= 0) & (x < nx) & (y >= 0) & (y < ny)

    def remote(src, dst, send, recv, dx, dy):
        return pltpu.make_async_remote_copy(
            src_ref=src, dst_ref=dst, send_sem=send, recv_sem=recv,
            device_id={"gx": ix + dx, "gy": iy + dy}, device_id_type=MESH,
        )

    column = {0: 0, 1: 1, -1: 2}
    coef_rows = {1: (rows, 0, HALO), -1: (HALO, HALO + rows, HALO), 0: (HALO, HALO, rows)}
    half = ext // 2
    half_rows = {1: (half, 0, half), -1: (0, half, half), 0: (0, 0, ext)}

    def coef_copy(number, dx, dy):
        src, dst, size = coef_rows[dx]
        return remote(
            coef.at[0, :, :, pl.ds(src, size)], coef.at[column[dy], :, :, pl.ds(dst, size)],
            c_send.at[number], c_recv.at[number], dx, dy,
        )

    def g_copy(number, dx, dy):
        src, dst, size = half_rows[dx]
        if dy == 0:
            src_ref, dst_ref = gx_out.at[:, pl.ds(src, size)], gx_in.at[:, pl.ds(dst, size)]
        else:
            slot = column[dy] - 1
            src_ref = gy_out.at[slot, :, pl.ds(src, size)]
            dst_ref = gy_in.at[slot + (2 if dx else 0), :, pl.ds(dst, size)]
        return remote(src_ref, dst_ref, g_send.at[number], g_recv.at[number], dx, dy)

    def start_all(make):
        for number, (dx, dy) in enumerate(sides):
            @pl.when(present(dx, dy))
            def _():
                make(number, dx, dy).start()

    def wait_recv_all(make):
        for number, (dx, dy) in enumerate(sides):
            @pl.when(present(-dx, -dy))
            def _():
                make(number, dx, dy).wait_recv()

    def wait_send_all(make):
        for number, (dx, dy) in enumerate(sides):
            @pl.when(present(dx, dy))
            def _():
                make(number, dx, dy).wait_send()

    start_all(coef_copy)

    def wrapped(shape, dim):
        lane = iota(shape, dim)
        return jnp.where(lane < wide - wide // 4, lane, lane - wide)

    a_shape = (steps * ext, steps * fine_x)
    a_row, a_col = iota(a_shape, 0), iota(a_shape, 1)
    a_same = a_row // ext == a_col // fine_x
    a_base = 0.25 * (a_col % fine_x - 4 * (a_row % ext - HALO)).astype(F32)
    a_base = jnp.where(a_same, a_base, 1e6)
    c_shape = (fine_y, wide)
    c_base = 0.25 * (iota(c_shape, 0) - 4 * wrapped(c_shape, 1)).astype(F32)

    def tent(base, offset):
        return jnp.maximum(0.5 - jnp.abs(base - (offset.astype(F32) + 0.5) * 0.25), 0.0).astype(BF16)

    restricted = []
    for level in range(levels):
        fine = inn[:, level].reshape(steps * fine_x, fine_y)
        part = dot(tent(a_base, r_off[level, 0]), fine)
        restricted.append(split_dot(part, tent(c_base, r_off[level, 1])))

    def at_time(t):
        return jnp.concatenate([r[t * ext : (t + 1) * ext] for r in restricted], axis=0)

    wait_recv_all(coef_copy)
    lane = iota((levels * ext, cols), 1)
    low, high = lane < HALO, lane >= cols - HALO

    def extended(field):
        own, left, right = (coef[c, field].reshape(levels * ext, cols) for c in range(3))
        rim = jnp.where(low, right, jnp.where(high, left, 0.0))
        return jnp.concatenate([own, rim], axis=1)

    e, n, w_obs = extended(0), extended(1), extended(2)
    stay = 1.0 - e - n
    total_rows = levels * ext

    def forward(x):
        return stay * x + e * pltpu.roll(x, 1, 0) + n * pltpu.roll(x, 1, 1)

    def adjoint(y):
        return stay * y + pltpu.roll(e * y, total_rows - 1, 0) + pltpu.roll(n * y, wide - 1, 1)

    lam = w_obs * at_time(steps - 1)
    for t in range(steps - 2, -1, -1):
        lam = adjoint(lam) + w_obs * at_time(t)
    mine = adjoint(lam)
    near, far = mine[:, :cols], mine[:, cols:]
    gx_out[...] = mine.reshape(levels, ext, wide)
    gy_out[0] = jnp.where(low, far, near).reshape(levels, ext, cols)
    gy_out[1] = jnp.where(low, near, far).reshape(levels, ext, cols)
    start_all(g_copy)

    m_shape = (total_rows, wide)
    m_row = iota(m_shape, 0) % ext - HALO + ix * rows
    m_col = wrapped(m_shape, 1) + iy * cols
    inside = (m_row >= 0) & (m_row < nx * rows) & (m_col >= 0) & (m_col < ny * cols)

    wait_recv_all(g_copy)
    from_left = (gy_in[0] + gy_in[2]).reshape(total_rows, cols)
    from_right = (gy_in[1] + gy_in[3]).reshape(total_rows, cols)
    near_rim = jnp.where(low, from_left, jnp.where(high, from_right, 0.0))
    far_rim = jnp.where(low, from_right, jnp.where(high, from_left, 0.0))
    beside = gx_in[...].reshape(total_rows, wide)
    g = mine + beside + jnp.concatenate([near_rim, far_rim], axis=1)
    g = jnp.where(inside, g, 0.0)

    def hessian(p):
        states = []
        state = p
        for _ in range(steps):
            state = forward(state)
            states.append(state)
        lam = w_obs * states[-1]
        for t in range(steps - 2, -1, -1):
            lam = adjoint(lam) + w_obs * states[t]
        return p + adjoint(lam)

    w = jnp.where(inside, hessian(g), 0.0)
    v = hessian(w)

    def own(x):
        return [x[l * ext + HALO : l * ext + HALO + rows, :cols] for l in range(levels)]

    g_own, w_own, v_own = own(g), own(w), own(v)

    def partial(a, b):
        return sum(jnp.sum(x * y, axis=0, keepdims=True) for x, y in zip(a, b))

    gram = jnp.concatenate(
        [partial(g_own, g_own), partial(g_own, w_own), partial(w_own, w_own), partial(w_own, v_own)]
        + [jnp.zeros((4, cols), F32)], axis=0,
    )
    red[me] = gram

    def red_send(k):
        return pltpu.make_async_remote_copy(
            src_ref=red.at[me], dst_ref=red.at[me], send_sem=r_send.at[k], recv_sem=r_recv.at[me],
            device_id=peer(k), device_id_type=MESH,
        )

    def red_recv(k):
        other = lax.rem(me + k, group)
        return pltpu.make_async_remote_copy(
            src_ref=red.at[me], dst_ref=red.at[other], send_sem=r_send.at[k],
            recv_sem=r_recv.at[other], device_id=peer(k), device_id_type=MESH,
        )

    repeat(group, lambda k: red_send(k).start())

    q_shape = (wide, fine_y)
    q_base = 0.25 * iota(q_shape, 1).astype(F32) - wrapped(q_shape, 0).astype(F32)
    b_shape = (fine_x, 2 * ext)
    b_base = 0.25 * iota(b_shape, 0).astype(F32) - (iota(b_shape, 1) % ext - HALO).astype(F32)

    def hat(base, offset):
        return jnp.maximum(1.0 - jnp.abs(base - offset.astype(F32) * 0.25), 0.0).astype(BF16)

    fine_parts = []
    for level in range(levels):
        both = jnp.concatenate([x[level * ext : (level + 1) * ext] for x in (g, w)], axis=0)
        across = split_dot(both, hat(q_base, p_off[level, 1]))
        up = hat(b_base, p_off[level, 0])
        fine_parts.append([
            dot(up, jnp.concatenate(split(across[k * ext : (k + 1) * ext]), axis=0)) for k in range(2)
        ])

    repeat(group, lambda k: red_recv(k).wait_recv())
    sums = jnp.sum(jnp.sum(red[...], axis=0), axis=1, keepdims=True)
    gg, gw, ww, wv = (sums[k : k + 1] for k in range(4))
    alpha = gg / gw
    rr = gg - 2.0 * alpha * gw + alpha * alpha * ww
    beta = rr / gg
    more = 1.0 + beta
    curvature = more * more * gw - 2.0 * alpha * more * ww + alpha * alpha * wv
    alpha_1 = rr / curvature
    from_g = alpha + alpha_1 * more
    from_w = -alpha_1 * alpha
    res_w = -(alpha + alpha_1 * more)
    res_v = alpha_1 * alpha
    for level in range(levels):
        out[level] = from_g * fine_parts[level][0] + from_w * fine_parts[level][1]
        res[level] = g_own[level] + res_w * w_own[level] + res_v * v_own[level]

    wait_send_all(coef_copy)
    wait_send_all(g_copy)
    repeat(group, lambda k: red_send(k).wait_send())


def on_device(sizes, innovations, restrict_offsets, prolong_offsets, east, north, weight):
    _, levels, fine_x, fine_y = innovations.shape
    rows, cols = fine_x // 4, fine_y // 4
    ext = rows + 2 * HALO
    group = sizes[0] * sizes[1] * sizes[2]
    vmem = pl.BlockSpec(memory_space=pltpu.VMEM)
    smem = pl.BlockSpec(memory_space=pltpu.SMEM)
    dma = pltpu.SemaphoreType.DMA
    return pl.pallas_call(
        functools.partial(kernel, sizes),
        out_shape=(
            jax.ShapeDtypeStruct((levels, fine_x, fine_y), F32),
            jax.ShapeDtypeStruct((levels, rows, cols), F32),
        ),
        in_specs=[vmem, smem, smem, vmem, vmem, vmem],
        out_specs=(vmem, vmem),
        scratch_shapes=[
            pltpu.VMEM((3, 3, levels, ext, cols), F32),
            pltpu.VMEM((levels, ext, 2 * cols), F32),
            pltpu.VMEM((4, levels, ext, cols), F32),
            pltpu.VMEM((levels, ext, 2 * cols), F32),
            pltpu.VMEM((2, levels, ext, cols), F32),
            pltpu.VMEM((group, 8, cols), F32),
            dma((8,)), dma((8,)), dma((8,)), dma((8,)), dma((group,)), dma((group,)),
        ],
        compiler_params=pltpu.CompilerParams(
            collective_id=0, has_side_effects=True, vmem_limit_bytes=32 * 1024 * 1024
        ),
    )(innovations, restrict_offsets, prolong_offsets, east, north, weight)


def solution(mesh):
    sizes = tuple(mesh.shape[axis] for axis in ("gx", "gy", "lev"))
    inner = P(("ens", "lev"), "gx", "gy")
    in_specs = (P("ens", "lev", "gx", "gy"), P("lev", None), P("lev", None), inner, inner, inner)
    return jax.shard_map(
        functools.partial(on_device, sizes), mesh=mesh, in_specs=in_specs,
        out_specs=(inner, inner), check_vma=False,
    )
```

time: 295 us -> 26.5 us (0.09)
  starting transfers between devices: 99.1 us -> 0 us
  blocking collectives: 93.4 us -> 0 us
  waiting for transfers between devices: 81.6 us -> 0 us
  Pallas kernels: 0 us -> 19.6 us
  other arithmetic: 6.11 us -> 0 us
  between operations: 5.74 us -> 0.65 us
  matrix products: 3.24 us -> 0 us
    ppermute x48 -> x0, starting transfers between devices: 99.1 us -> none  [the longest x40 83 us: from_behind(): return lax.ppermute(block, axis, route)]
    psum x3 -> x0, blocking collectives: 93.4 us -> none  [grand_total(): return lax.psum((values[0],), ('gx', 'gy', 'lev'))]
    ppermute x48 -> x0, waiting for transfers between devices: 81.6 us -> none  [the longest x40 64.1 us: from_behind(): return lax.ppermute(block, axis, route)]
    pallas_call x0 -> x1, Pallas kernels: none -> 19.6 us  [on_device(): pl.pallas_call(functools.partial(kernel, sizes), out_shape=(jax.ShapeDtyp...]
    unnamed x10 -> x14, local copies, waits for them, and re-layouts: 0.02 us -> 5.85 us
    slice x79 -> x0, local copies, waits for them, and re-layouts: 4.7 us -> none  [the longest x3 1.04 us: extended_2(): last = lax.slice_in_dim(shard, length - width, length, axis=dim)]
    dot_general x4 -> x0, matrix products: 3.24 us -> none  [the longest x1 1.38 us: on_device(): jnp.einsum('lfm,lgm->lfg', half_done, cols_prolong, precision=lax.Precisi...]
  transfers between devices with their start and end apart: 48 -> 0, of which waited for: 28 -> 0; matrix products, arithmetic and copies ran while one was open for 1% -> 0% of each run, Pallas kernels for 0% -> 0%
where the time goes in v1:
time: 26.5 us; the launch traced here: 26.1 us
  Pallas kernels  19.6 us (74%)
  local copies, waits for them, and re-layouts  5.85 us (22%)
  between operations  0.65 us (2%)
    pallas_call x1, Pallas kernels, on_device(): pl.pallas_call(functools.partial(kernel, sizes), out_shape=(jax.ShapeDtyp...  19.6 us
    unnamed x14, local copies, waits for them, and re-layouts  5.85 us

profile of v1, /device:TPU:0, one launch (start us, length us, event | category | flops | bytes accessed | tf_op | source)
XLA Modules:
  0.0 26.1 jit_solution(12042064087420402328)
XLA Ops:
  0.6 0.0 copy-start
  0.6 1.0 %copy-done = bf16[4,2,64,512]{3,2,1,0:T(8,128)(2,1)S(1)} copy-done((bf16[4,2,64,512]{3,2,1,0:T(8,128)(2,1)S(1)}, bf16[4,2,64,512]{3,2,1,0:T(8,128)(2,1)}, u32[]{:S(2)}) %copy-start) | copy-done | bytes 524312
  1.7 0.0 copy-start.1
  1.7 0.7 %copy-done.1 = f32[2,16,128]{2,1,0:T(8,128)S(1)} copy-done((f32[2,16,128]{2,1,0:T(8,128)S(1)}, f32[2,16,128]{2,1,0:T(8,128)}, u32[]{:S(2)}) %copy-start.1) | copy-done | bytes 16408
  2.4 0.0 copy-start.2
  2.4 0.7 %copy-done.2 = f32[2,16,128]{2,1,0:T(8,128)S(1)} copy-done((f32[2,16,128]{2,1,0:T(8,128)S(1)}, f32[2,16,128]{2,1,0:T(8,128)}, u32[]{:S(2)}) %copy-start.2) | copy-done | bytes 16408
  3.1 0.0 copy-start.3
  3.1 0.7 %copy-done.3 = f32[2,16,128]{2,1,0:T(8,128)S(1)} copy-done((f32[2,16,128]{2,1,0:T(8,128)S(1)}, f32[2,16,128]{2,1,0:T(8,128)}, u32[]{:S(2)}) %copy-start.3) | copy-done | bytes 16408
  3.8 0.0 copy-start.4
  3.8 0.7 %copy-done.4 = s32[2,2]{1,0:T(2,128)S(1)} copy-done((s32[2,2]{1,0:T(2,128)S(1)}, s32[2,2]{1,0:T(2,128)}, u32[]{:S(2)}) %copy-start.4) | copy-done | bytes 40
  4.5 0.0 copy-start.5
  4.5 0.7 %copy-done.5 = s32[2,2]{1,0:T(2,128)S(1)} copy-done((s32[2,2]{1,0:T(2,128)S(1)}, s32[2,2]{1,0:T(2,128)}, u32[]{:S(2)}) %copy-start.5) | copy-done | bytes 40
  5.2 19.6 %shard_map.77 = (f32[2,64,512]{2,1,0:T(8,128)S(1)}, f32[2,16,128]{2,1,0:T(8,128)S(1)}) custom-call(bf16[4,2,64,512]{3,2,1,0:T(8,128)(2,1)S(1)} %copy-done, s32[2,2]{1,0:T(2,128)S(1)} %copy-done.4, s32[2,2]{1,0:T(2,128)S(1)} %copy-done.5, f32[2,16,128]{2,1,0:T(8,128)S(1)} %copy-done.1, f32[2,16,128]{2,1,0:T(8,128)S(1)} %copy-done.2, f32[2,16,128]{2,1,0:T(8,128)S(1)} %copy-done.3), custom_call_target="tpu_custom_call" | custom-call | tf_op jit(solution)/shard_map/pallas_call | solution.py:283
  24.8 0.7 %copy.10 = f32[2,64,512]{2,1,0:T(8,128)} copy(f32[2,64,512]{2,1,0:T(8,128)S(1)} %get-tuple-element.4) | data formatting | bytes 524288
  25.5 0.6 %copy.11 = f32[2,16,128]{2,1,0:T(8,128)} copy(f32[2,16,128]{2,1,0:T(8,128)S(1)} %get-tuple-element.5) | data formatting | bytes 32768
Async XLA Ops:
  0.6 1.0 %copy-start = (bf16[4,2,64,512]{3,2,1,0:T(8,128)(2,1)S(1)}, bf16[4,2,64,512]{3,2,1,0:T(8,128)(2,1)}, u32[]{:S(2)}) copy-start(bf16[4,2,64,512]{3,2,1,0:T(8,128)(2,1)} %inn.1) | copy-start | bytes 1572868
  1.7 0.7 %copy-start.1 = (f32[2,16,128]{2,1,0:T(8,128)S(1)}, f32[2,16,128]{2,1,0:T(8,128)}, u32[]{:S(2)}) copy-start(f32[2,16,128]{2,1,0:T(8,128)} %east.1) | copy-start | bytes 49156
  2.4 0.7 %copy-start.2 = (f32[2,16,128]{2,1,0:T(8,128)S(1)}, f32[2,16,128]{2,1,0:T(8,128)}, u32[]{:S(2)}) copy-start(f32[2,16,128]{2,1,0:T(8,128)} %north.1) | copy-start | bytes 49156
  3.1 0.7 %copy-start.3 = (f32[2,16,128]{2,1,0:T(8,128)S(1)}, f32[2,16,128]{2,1,0:T(8,128)}, u32[]{:S(2)}) copy-start(f32[2,16,128]{2,1,0:T(8,128)} %weight.1) | copy-start | bytes 49156
  3.8 0.7 %copy-start.4 = (s32[2,2]{1,0:T(2,128)S(1)}, s32[2,2]{1,0:T(2,128)}, u32[]{:S(2)}) copy-start(s32[2,2]{1,0:T(2,128)} %r_off.1) | copy-start | bytes 52
  4.5 0.7 %copy-start.5 = (s32[2,2]{1,0:T(2,128)S(1)}, s32[2,2]{1,0:T(2,128)}, u32[]{:S(2)}) copy-start(s32[2,2]{1,0:T(2,128)} %p_off.1) | copy-start | bytes 52

commit v2 on v1

--- a/solution.py
+++ b/solution.py
@@ -39,8 +39,8 @@
 
 
 def kernel(
-    sizes, inn, r_off, p_off, east, north, weight, out, res, coef, gx_in, gy_in, gx_out, gy_out,
-    red, c_send, c_recv, g_send, g_recv, r_send, r_recv,
+    sizes, inn_hbm, r_hbm, p_hbm, east, north, weight, out, res, inn, r_off, p_off, coef, gx_in, gy_in, gx_out, gy_out,
+    red, local, c_send, c_recv, g_send, g_recv, r_send, r_recv,
 ):
     nx, ny, nl = sizes
     group = nx * ny * nl
@@ -59,14 +59,45 @@
             "lev": lax.rem(other, nl),
         }
 
-    coef[...] = jnp.zeros_like(coef)
+    loads = [
+        pltpu.make_async_copy(src, dst, local.at[k])
+        for k, (src, dst) in enumerate(
+            [(ref, coef.at[0, field, :, pl.ds(HALO, rows)]) for field, ref in enumerate((east, north, weight))]
+            + [(r_hbm, r_off), (inn_hbm, inn), (p_hbm, p_off)]
+        )
+    ]
+    for load in loads:
+        load.start()
+    edge = jnp.zeros((3, levels, HALO, cols), F32)
+    coef[0, :, :, :HALO] = edge
+    coef[0, :, :, HALO + rows :] = edge
+    coef[1:] = jnp.zeros((2, 3, levels, ext, cols), F32)
     gx_in[...] = jnp.zeros_like(gx_in)
     gy_in[...] = jnp.zeros_like(gy_in)
-    for field, ref in enumerate((east, north, weight)):
-        coef[0, field, :, HALO : HALO + rows, :] = ref[...]
     barrier = pltpu.get_barrier_semaphore()
     repeat(group, lambda k: pl.semaphore_signal(barrier, inc=1, device_id=peer(k), device_id_type=MESH))
+    def wrapped(shape, dim):
+        lane = iota(shape, dim)
+        return jnp.where(lane < wide - wide // 4, lane, lane - wide)
+
+    a_shape = (steps * ext, steps * fine_x)
+    a_row, a_col = iota(a_shape, 0), iota(a_shape, 1)
+    a_same = a_row // ext == a_col // fine_x
+    a_base = 0.25 * (a_col % fine_x - 4 * (a_row % ext - HALO)).astype(F32)
+    a_base = jnp.where(a_same, a_base, 1e6)
+    c_shape = (fine_y, wide)
+    c_base = 0.25 * (iota(c_shape, 0) - 4 * wrapped(c_shape, 1)).astype(F32)
+
+    def tent(base, offset):
+        return jnp.maximum(0.5 - jnp.abs(base - (offset.astype(F32) + 0.5) * 0.25), 0.0).astype(BF16)
+
+    loads[3].wait()
+    a_mats = [tent(a_base, r_off[level, 0]) for level in range(levels)]
+    c_mats = [tent(c_base, r_off[level, 1]) for level in range(levels)]
+
     pl.semaphore_wait(barrier, group - 1)
+    for load in loads[:3]:
+        load.wait()
 
     sides = [(dx, dy) for dx in (0, 1, -1) for dy in (0, 1, -1) if (dx, dy) != (0, 0)]
     sides = [(dx, dy) for dx, dy in sides if (nx > 1 or not dx) and (ny > 1 or not dy)]
@@ -123,26 +154,12 @@
 
     start_all(coef_copy)
 
-    def wrapped(shape, dim):
-        lane = iota(shape, dim)
-        return jnp.where(lane < wide - wide // 4, lane, lane - wide)
-
-    a_shape = (steps * ext, steps * fine_x)
-    a_row, a_col = iota(a_shape, 0), iota(a_shape, 1)
-    a_same = a_row // ext == a_col // fine_x
-    a_base = 0.25 * (a_col % fine_x - 4 * (a_row % ext - HALO)).astype(F32)
-    a_base = jnp.where(a_same, a_base, 1e6)
-    c_shape = (fine_y, wide)
-    c_base = 0.25 * (iota(c_shape, 0) - 4 * wrapped(c_shape, 1)).astype(F32)
-
-    def tent(base, offset):
-        return jnp.maximum(0.5 - jnp.abs(base - (offset.astype(F32) + 0.5) * 0.25), 0.0).astype(BF16)
-
+    loads[4].wait()
     restricted = []
     for level in range(levels):
         fine = inn[:, level].reshape(steps * fine_x, fine_y)
-        part = dot(tent(a_base, r_off[level, 0]), fine)
-        restricted.append(split_dot(part, tent(c_base, r_off[level, 1])))
+        part = dot(a_mats[level], fine)
+        restricted.append(split_dot(part, c_mats[level]))
 
     def at_time(t):
         return jnp.concatenate([r[t * ext : (t + 1) * ext] for r in restricted], axis=0)
@@ -241,6 +258,7 @@
     def hat(base, offset):
         return jnp.maximum(1.0 - jnp.abs(base - offset.astype(F32) * 0.25), 0.0).astype(BF16)
 
+    loads[5].wait()
     fine_parts = []
     for level in range(levels):
         both = jnp.concatenate([x[level * ext : (level + 1) * ext] for x in (g, w)], axis=0)
@@ -278,7 +296,7 @@
     ext = rows + 2 * HALO
     group = sizes[0] * sizes[1] * sizes[2]
     vmem = pl.BlockSpec(memory_space=pltpu.VMEM)
-    smem = pl.BlockSpec(memory_space=pltpu.SMEM)
+    hbm = pl.BlockSpec(memory_space=pltpu.HBM)
     dma = pltpu.SemaphoreType.DMA
     return pl.pallas_call(
         functools.partial(kernel, sizes),
@@ -286,16 +304,19 @@
             jax.ShapeDtypeStruct((levels, fine_x, fine_y), F32),
             jax.ShapeDtypeStruct((levels, rows, cols), F32),
         ),
-        in_specs=[vmem, smem, smem, vmem, vmem, vmem],
+        in_specs=[hbm] * 6,
         out_specs=(vmem, vmem),
         scratch_shapes=[
+            pltpu.VMEM(innovations.shape, BF16),
+            pltpu.SMEM((levels, 2), jnp.int32),
+            pltpu.SMEM((levels, 2), jnp.int32),
             pltpu.VMEM((3, 3, levels, ext, cols), F32),
             pltpu.VMEM((levels, ext, 2 * cols), F32),
             pltpu.VMEM((4, levels, ext, cols), F32),
             pltpu.VMEM((levels, ext, 2 * cols), F32),
             pltpu.VMEM((2, levels, ext, cols), F32),
             pltpu.VMEM((group, 8, cols), F32),
-            dma((8,)), dma((8,)), dma((8,)), dma((8,)), dma((group,)), dma((group,)),
+            dma((6,)), dma((8,)), dma((8,)), dma((8,)), dma((8,)), dma((group,)), dma((group,)),
         ],
         compiler_params=pltpu.CompilerParams(
             collective_id=0, has_side_effects=True, vmem_limit_bytes=32 * 1024 * 1024

time: 26.5 us -> 26.1 us (0.985)
  Pallas kernels: 19.6 us -> 19.1 us
    pallas_call x1, Pallas kernels: 19.6 us -> 19.1 us  [on_device(): pl.pallas_call(functools.partial(kernel, sizes), out_shape=(jax.ShapeDtyp...]
where the time goes in v2:
time: 26.1 us; the launch traced here: 25.6 us
  Pallas kernels  19.1 us (73%)
  local copies, waits for them, and re-layouts  5.85 us (22%)
  between operations  0.65 us (2%)
    pallas_call x1, Pallas kernels, on_device(): pl.pallas_call(functools.partial(kernel, sizes), out_shape=(jax.ShapeDtyp...  19.1 us
    unnamed x14, local copies, waits for them, and re-layouts  5.85 us

profile of v2, /device:TPU:0, one launch (start us, length us, event | category | flops | bytes accessed | tf_op | source)
XLA Modules:
  0.0 25.6 jit_solution(2330726456374788355)
XLA Ops:
  0.6 0.0 copy-start
  0.6 1.0 %copy-done = bf16[4,2,64,512]{3,2,1,0:T(8,128)(2,1)S(1)} copy-done((bf16[4,2,64,512]{3,2,1,0:T(8,128)(2,1)S(1)}, bf16[4,2,64,512]{3,2,1,0:T(8,128)(2,1)}, u32[]{:S(2)}) %copy-start) | copy-done | bytes 524312
  1.7 0.0 copy-start.1
  1.7 0.7 %copy-done.1 = f32[2,16,128]{2,1,0:T(8,128)S(1)} copy-done((f32[2,16,128]{2,1,0:T(8,128)S(1)}, f32[2,16,128]{2,1,0:T(8,128)}, u32[]{:S(2)}) %copy-start.1) | copy-done | bytes 16408
  2.4 0.0 copy-start.2
  2.4 0.7 %copy-done.2 = f32[2,16,128]{2,1,0:T(8,128)S(1)} copy-done((f32[2,16,128]{2,1,0:T(8,128)S(1)}, f32[2,16,128]{2,1,0:T(8,128)}, u32[]{:S(2)}) %copy-start.2) | copy-done | bytes 16408
  3.1 0.0 copy-start.3
  3.1 0.7 %copy-done.3 = f32[2,16,128]{2,1,0:T(8,128)S(1)} copy-done((f32[2,16,128]{2,1,0:T(8,128)S(1)}, f32[2,16,128]{2,1,0:T(8,128)}, u32[]{:S(2)}) %copy-start.3) | copy-done | bytes 16408
  3.8 0.0 copy-start.4
  3.8 0.7 %copy-done.4 = s32[2,2]{1,0:T(2,128)S(1)} copy-done((s32[2,2]{1,0:T(2,128)S(1)}, s32[2,2]{1,0:T(2,128)}, u32[]{:S(2)}) %copy-start.4) | copy-done | bytes 40
  4.5 0.0 copy-start.5
  4.5 0.7 %copy-done.5 = s32[2,2]{1,0:T(2,128)S(1)} copy-done((s32[2,2]{1,0:T(2,128)S(1)}, s32[2,2]{1,0:T(2,128)}, u32[]{:S(2)}) %copy-start.5) | copy-done | bytes 40
  5.2 19.1 %shard_map.77 = (f32[2,64,512]{2,1,0:T(8,128)S(1)}, f32[2,16,128]{2,1,0:T(8,128)S(1)}) custom-call(bf16[4,2,64,512]{3,2,1,0:T(8,128)(2,1)S(1)} %copy-done, s32[2,2]{1,0:T(2,128)S(1)} %copy-done.4, s32[2,2]{1,0:T(2,128)S(1)} %copy-done.5, f32[2,16,128]{2,1,0:T(8,128)S(1)} %copy-done.1, f32[2,16,128]{2,1,0:T(8,128)S(1)} %copy-done.2, f32[2,16,128]{2,1,0:T(8,128)S(1)} %copy-done.3), custom_call_target="tpu_custom_call" | custom-call | tf_op jit(solution)/shard_map/pallas_call | solution.py:301
  24.3 0.7 %copy.10 = f32[2,64,512]{2,1,0:T(8,128)} copy(f32[2,64,512]{2,1,0:T(8,128)S(1)} %get-tuple-element.4) | data formatting | bytes 524288
  25.0 0.6 %copy.11 = f32[2,16,128]{2,1,0:T(8,128)} copy(f32[2,16,128]{2,1,0:T(8,128)S(1)} %get-tuple-element.5) | data formatting | bytes 32768
Async XLA Ops:
  0.6 1.0 %copy-start = (bf16[4,2,64,512]{3,2,1,0:T(8,128)(2,1)S(1)}, bf16[4,2,64,512]{3,2,1,0:T(8,128)(2,1)}, u32[]{:S(2)}) copy-start(bf16[4,2,64,512]{3,2,1,0:T(8,128)(2,1)} %inn_hbm.1) | copy-start | bytes 1572868
  1.7 0.7 %copy-start.1 = (f32[2,16,128]{2,1,0:T(8,128)S(1)}, f32[2,16,128]{2,1,0:T(8,128)}, u32[]{:S(2)}) copy-start(f32[2,16,128]{2,1,0:T(8,128)} %east.1) | copy-start | bytes 49156
  2.4 0.7 %copy-start.2 = (f32[2,16,128]{2,1,0:T(8,128)S(1)}, f32[2,16,128]{2,1,0:T(8,128)}, u32[]{:S(2)}) copy-start(f32[2,16,128]{2,1,0:T(8,128)} %north.1) | copy-start | bytes 49156
  3.1 0.7 %copy-start.3 = (f32[2,16,128]{2,1,0:T(8,128)S(1)}, f32[2,16,128]{2,1,0:T(8,128)}, u32[]{:S(2)}) copy-start(f32[2,16,128]{2,1,0:T(8,128)} %weight.1) | copy-start | bytes 49156
  3.8 0.7 %copy-start.4 = (s32[2,2]{1,0:T(2,128)S(1)}, s32[2,2]{1,0:T(2,128)}, u32[]{:S(2)}) copy-start(s32[2,2]{1,0:T(2,128)} %r_hbm.1) | copy-start | bytes 52
  4.5 0.7 %copy-start.5 = (s32[2,2]{1,0:T(2,128)S(1)}, s32[2,2]{1,0:T(2,128)}, u32[]{:S(2)}) copy-start(s32[2,2]{1,0:T(2,128)} %p_hbm.1) | copy-start | bytes 52

commit v3 on v2

--- a/solution.py
+++ b/solution.py
@@ -9,6 +9,7 @@
 
 MESH = pl.DeviceIdType.MESH
 HALO = 8
+SIDES = tuple((dx, dy) for dx in (0, 1, -1) for dy in (0, 1, -1) if dx or dy)
 F32, BF16 = jnp.float32, jnp.bfloat16
 
 
@@ -39,7 +40,7 @@
 
 
 def kernel(
-    sizes, inn_hbm, r_hbm, p_hbm, east, north, weight, out, res, inn, r_off, p_off, coef, gx_in, gy_in, gx_out, gy_out,
+    sizes, inn_hbm, r_hbm, p_hbm, east, north, weight, out, res, inn, r_off, p_off, coef, c_rim, c_pack, g_near, g_rim, g_pack, near_out,
     red, local, c_send, c_recv, g_send, g_recv, r_send, r_recv,
 ):
     nx, ny, nl = sizes
@@ -62,18 +63,17 @@
     loads = [
         pltpu.make_async_copy(src, dst, local.at[k])
         for k, (src, dst) in enumerate(
-            [(ref, coef.at[0, field, :, pl.ds(HALO, rows)]) for field, ref in enumerate((east, north, weight))]
+            [(ref, coef.at[field, :, pl.ds(HALO, rows)]) for field, ref in enumerate((east, north, weight))]
             + [(r_hbm, r_off), (inn_hbm, inn), (p_hbm, p_off)]
         )
     ]
     for load in loads:
         load.start()
     edge = jnp.zeros((3, levels, HALO, cols), F32)
-    coef[0, :, :, :HALO] = edge
-    coef[0, :, :, HALO + rows :] = edge
-    coef[1:] = jnp.zeros((2, 3, levels, ext, cols), F32)
-    gx_in[...] = jnp.zeros_like(gx_in)
-    gy_in[...] = jnp.zeros_like(gy_in)
+    coef[:, :, :HALO] = edge
+    coef[:, :, HALO + rows :] = edge
+    for ref in (c_rim, g_near, g_rim):
+        ref[...] = jnp.zeros_like(ref)
     barrier = pltpu.get_barrier_semaphore()
     repeat(group, lambda k: pl.semaphore_signal(barrier, inc=1, device_id=peer(k), device_id_type=MESH))
     def wrapped(shape, dim):
@@ -99,9 +99,6 @@
     for load in loads[:3]:
         load.wait()
 
-    sides = [(dx, dy) for dx in (0, 1, -1) for dy in (0, 1, -1) if (dx, dy) != (0, 0)]
-    sides = [(dx, dy) for dx, dy in sides if (nx > 1 or not dx) and (ny > 1 or not dy)]
-
     def present(dx, dy):
         x, y = ix + dx, iy + dy
         return (x >= 0) & (x < nx) & (y >= 0) & (y < ny)
@@ -112,47 +109,82 @@
             device_id={"gx": ix + dx, "gy": iy + dy}, device_id_type=MESH,
         )
 
-    column = {0: 0, 1: 1, -1: 2}
-    coef_rows = {1: (rows, 0, HALO), -1: (HALO, HALO + rows, HALO), 0: (HALO, HALO, rows)}
     half = ext // 2
-    half_rows = {1: (half, 0, half), -1: (0, half, half), 0: (0, 0, ext)}
-
-    def coef_copy(number, dx, dy):
-        src, dst, size = coef_rows[dx]
-        return remote(
-            coef.at[0, :, :, pl.ds(src, size)], coef.at[column[dy], :, :, pl.ds(dst, size)],
-            c_send.at[number], c_recv.at[number], dx, dy,
-        )
-
-    def g_copy(number, dx, dy):
-        src, dst, size = half_rows[dx]
+    coef_rows = {1: (rows, 0), -1: (HALO, HALO + rows)}
+    half_rows = {1: (half, 0), -1: (0, half)}
+
+    def coef_copies(number, dx, dy):
+        sems = c_send.at[number], c_recv.at[number]
+        if dy:
+            return [remote(c_pack, c_rim.at[number], *sems, dx, dy)]
+        src, dst = coef_rows[dx]
+        return [remote(coef.at[:, :, pl.ds(src, HALO)], coef.at[:, :, pl.ds(dst, HALO)], *sems, dx, dy)]
+
+    def g_copies(number, dx, dy):
+        slot = {1: 0, -1: 1, 0: 2}[dy]
+        found = [remote(g_pack.at[slot], g_rim.at[number], g_send.at[number], g_recv.at[number], dx, dy)]
         if dy == 0:
-            src_ref, dst_ref = gx_out.at[:, pl.ds(src, size)], gx_in.at[:, pl.ds(dst, size)]
-        else:
-            slot = column[dy] - 1
-            src_ref = gy_out.at[slot, :, pl.ds(src, size)]
-            dst_ref = gy_in.at[slot + (2 if dx else 0), :, pl.ds(dst, size)]
-        return remote(src_ref, dst_ref, g_send.at[number], g_recv.at[number], dx, dy)
+            src, dst = half_rows[dx]
+            extra = len(SIDES) + number
+            found.append(remote(
+                near_out.at[:, pl.ds(src, half)], g_near.at[:, pl.ds(dst, half)],
+                g_send.at[extra], g_recv.at[extra], dx, dy,
+            ))
+        return found
 
     def start_all(make):
-        for number, (dx, dy) in enumerate(sides):
+        for number, (dx, dy) in enumerate(SIDES):
             @pl.when(present(dx, dy))
             def _():
-                make(number, dx, dy).start()
+                for copy in make(number, dx, dy):
+                    copy.start()
 
     def wait_recv_all(make):
-        for number, (dx, dy) in enumerate(sides):
+        for number, (dx, dy) in enumerate(SIDES):
             @pl.when(present(-dx, -dy))
             def _():
-                make(number, dx, dy).wait_recv()
+                for copy in make(number, dx, dy):
+                    copy.wait_recv()
 
     def wait_send_all(make):
-        for number, (dx, dy) in enumerate(sides):
+        for number, (dx, dy) in enumerate(SIDES):
             @pl.when(present(dx, dy))
             def _():
-                make(number, dx, dy).wait_send()
-
-    start_all(coef_copy)
+                for copy in make(number, dx, dy):
+                    copy.wait_send()
+
+    tile_lane = iota((HALO, cols), 1)
+    window = (tile_lane + HALO) // (2 * HALO) % (cols // (2 * HALO))
+    upper = (tile_lane + HALO) % (2 * HALO) < HALO
+
+    def turn(tile, windows):
+        shift = windows * 2 * HALO % cols
+        return pltpu.roll(tile, shift, 1) if shift else tile
+
+    def pack(tiles):
+        packed = jnp.zeros((HALO, cols), F32)
+        for k, tile in enumerate(tiles):
+            packed = jnp.where(window == k, turn(tile, k), packed)
+        return packed
+
+    def unpack(packed, k):
+        return jnp.where(window == 0, turn(packed, -k), 0.0)
+
+    row_tiles = rows // HALO
+
+    def own_tiles(field):
+        return [
+            coef[field, level, HALO * (1 + r) : HALO * (2 + r), :]
+            for level in range(levels) for r in range(row_tiles)
+        ]
+
+    c_pack[0] = pack(own_tiles(0) + own_tiles(1))
+    c_pack[1] = pack(own_tiles(2))
+
+    def arrived(dx, dy):
+        return SIDES.index((-dx, -dy))
+
+    start_all(coef_copies)
 
     loads[4].wait()
     restricted = []
@@ -164,14 +196,21 @@
     def at_time(t):
         return jnp.concatenate([r[t * ext : (t + 1) * ext] for r in restricted], axis=0)
 
-    wait_recv_all(coef_copy)
-    lane = iota((levels * ext, cols), 1)
-    low, high = lane < HALO, lane >= cols - HALO
+    wait_recv_all(coef_copies)
+    rims = [
+        jnp.where(upper, c_rim[arrived(dx, -1)], c_rim[arrived(dx, 1)]) for dx in (-1, 0, 1)
+    ]
 
     def extended(field):
-        own, left, right = (coef[c, field].reshape(levels * ext, cols) for c in range(3))
-        rim = jnp.where(low, right, jnp.where(high, left, 0.0))
-        return jnp.concatenate([own, rim], axis=1)
+        part, first = field // 2, field % 2 * levels * row_tiles
+        far_tiles = []
+        for level in range(levels):
+            k = first + level * row_tiles
+            far_tiles.append(unpack(rims[0][part], k + row_tiles - 1))
+            far_tiles += [unpack(rims[1][part], k + r) for r in range(row_tiles)]
+            far_tiles.append(unpack(rims[2][part], k))
+        near = coef[field].reshape(levels * ext, cols)
+        return jnp.concatenate([near, jnp.concatenate(far_tiles, axis=0)], axis=1)
 
     e, n, w_obs = extended(0), extended(1), extended(2)
     stay = 1.0 - e - n
@@ -188,23 +227,39 @@
         lam = adjoint(lam) + w_obs * at_time(t)
     mine = adjoint(lam)
     near, far = mine[:, :cols], mine[:, cols:]
-    gx_out[...] = mine.reshape(levels, ext, wide)
-    gy_out[0] = jnp.where(low, far, near).reshape(levels, ext, cols)
-    gy_out[1] = jnp.where(low, near, far).reshape(levels, ext, cols)
-    start_all(g_copy)
+    tiles = total_rows // HALO
+    near_pack = pack([near[HALO * k : HALO * (k + 1)] for k in range(tiles)])
+    far_pack = pack([far[HALO * k : HALO * (k + 1)] for k in range(tiles)])
+    g_pack[0] = jnp.where(upper, near_pack, far_pack)
+    g_pack[1] = jnp.where(upper, far_pack, near_pack)
+    g_pack[2] = far_pack
+    near_out[...] = near.reshape(levels, ext, cols)
+    start_all(g_copies)
 
     m_shape = (total_rows, wide)
     m_row = iota(m_shape, 0) % ext - HALO + ix * rows
     m_col = wrapped(m_shape, 1) + iy * cols
     inside = (m_row >= 0) & (m_row < nx * rows) & (m_col >= 0) & (m_col < ny * cols)
 
-    wait_recv_all(g_copy)
-    from_left = (gy_in[0] + gy_in[2]).reshape(total_rows, cols)
-    from_right = (gy_in[1] + gy_in[3]).reshape(total_rows, cols)
-    near_rim = jnp.where(low, from_left, jnp.where(high, from_right, 0.0))
-    far_rim = jnp.where(low, from_right, jnp.where(high, from_left, 0.0))
-    beside = gx_in[...].reshape(total_rows, wide)
-    g = mine + beside + jnp.concatenate([near_rim, far_rim], axis=1)
+    wait_recv_all(g_copies)
+    ext_tiles = ext // HALO
+    first_half = window % ext_tiles < ext_tiles // 2
+
+    def shifted(dy):
+        back = turn(g_rim[arrived(-1, dy)], -(ext_tiles // 2))
+        ahead = turn(g_rim[arrived(1, dy)], ext_tiles // 2)
+        return jnp.where(first_half, back, ahead)
+
+    from_left = g_rim[arrived(0, -1)] + shifted(-1)
+    from_right = g_rim[arrived(0, 1)] + shifted(1)
+    near_rim = jnp.where(upper, from_right, from_left)
+    far_rim = jnp.where(upper, from_left, from_right) + shifted(0)
+
+    def unpack_all(packed):
+        return jnp.concatenate([unpack(packed, k) for k in range(tiles)], axis=0)
+
+    beside = g_near[...].reshape(total_rows, cols)
+    g = mine + jnp.concatenate([beside + unpack_all(near_rim), unpack_all(far_rim)], axis=1)
     g = jnp.where(inside, g, 0.0)
 
     def hessian(p):
@@ -233,7 +288,9 @@
         [partial(g_own, g_own), partial(g_own, w_own), partial(w_own, w_own), partial(w_own, v_own)]
         + [jnp.zeros((4, cols), F32)], axis=0,
     )
-    red[me] = gram
+    spread = jnp.sum(gram, axis=1, keepdims=True)
+    quarter = iota((8, cols), 1) // (cols // 4)
+    red[me] = jnp.sum(jnp.where(quarter == iota((8, cols), 0), spread, 0.0), axis=0, keepdims=True)
 
     def red_send(k):
         return pltpu.make_async_remote_copy(
@@ -269,8 +326,8 @@
         ])
 
     repeat(group, lambda k: red_recv(k).wait_recv())
-    sums = jnp.sum(jnp.sum(red[...], axis=0), axis=1, keepdims=True)
-    gg, gw, ww, wv = (sums[k : k + 1] for k in range(4))
+    sums = jnp.sum(red[...], axis=0)
+    gg, gw, ww, wv = (sums[:, k * (cols // 4)][:, None] for k in range(4))
     alpha = gg / gw
     rr = gg - 2.0 * alpha * gw + alpha * alpha * ww
     beta = rr / gg
@@ -285,8 +342,8 @@
         out[level] = from_g * fine_parts[level][0] + from_w * fine_parts[level][1]
         res[level] = g_own[level] + res_w * w_own[level] + res_v * v_own[level]
 
-    wait_send_all(coef_copy)
-    wait_send_all(g_copy)
+    wait_send_all(coef_copies)
+    wait_send_all(g_copies)
     repeat(group, lambda k: red_send(k).wait_send())
 
 
@@ -301,8 +358,8 @@
     return pl.pallas_call(
         functools.partial(kernel, sizes),
         out_shape=(
-            jax.ShapeDtypeStruct((levels, fine_x, fine_y), F32),
-            jax.ShapeDtypeStruct((levels, rows, cols), F32),
+            pltpu.VMEM((levels, fine_x, fine_y), F32),
+            pltpu.VMEM((levels, rows, cols), F32),
         ),
         in_specs=[hbm] * 6,
         out_specs=(vmem, vmem),
@@ -310,16 +367,18 @@
             pltpu.VMEM(innovations.shape, BF16),
             pltpu.SMEM((levels, 2), jnp.int32),
             pltpu.SMEM((levels, 2), jnp.int32),
-            pltpu.VMEM((3, 3, levels, ext, cols), F32),
-            pltpu.VMEM((levels, ext, 2 * cols), F32),
-            pltpu.VMEM((4, levels, ext, cols), F32),
-            pltpu.VMEM((levels, ext, 2 * cols), F32),
-            pltpu.VMEM((2, levels, ext, cols), F32),
-            pltpu.VMEM((group, 8, cols), F32),
-            dma((6,)), dma((8,)), dma((8,)), dma((8,)), dma((8,)), dma((group,)), dma((group,)),
+            pltpu.VMEM((3, levels, ext, cols), F32),
+            pltpu.VMEM((8, 2, HALO, cols), F32),
+            pltpu.VMEM((2, HALO, cols), F32),
+            pltpu.VMEM((levels, ext, cols), F32),
+            pltpu.VMEM((8, HALO, cols), F32),
+            pltpu.VMEM((3, HALO, cols), F32),
+            pltpu.VMEM((levels, ext, cols), F32),
+            pltpu.VMEM((group, 1, cols), F32),
+            dma((6,)), dma((8,)), dma((8,)), dma((16,)), dma((16,)), dma((group,)), dma((group,)),
         ],
         compiler_params=pltpu.CompilerParams(
-            collective_id=0, has_side_effects=True, vmem_limit_bytes=32 * 1024 * 1024
+            collective_id=0, has_side_effects=True
         ),
     )(innovations, restrict_offsets, prolong_offsets, east, north, weight)
 

time: 26.1 us -> 20.9 us (0.80); the launches traced: 25.6 us -> 20.7 us
  local copies, waits for them, and re-layouts: 5.85 us -> 1.31 us
  Pallas kernels: 19.1 us -> 18.8 us
    unnamed x14 -> x2, local copies, waits for them, and re-layouts: 5.85 us -> 1.31 us
    pallas_call x1, Pallas kernels: 19.1 us -> 18.8 us  [on_device(): pl.pallas_call(functools.partial(kernel, sizes), out_shape=(pltpu.VMEM((l...]
where the time goes in v3:
time: 20.9 us; the launch traced here: 20.7 us
  Pallas kernels  18.8 us (90%)
  local copies, waits for them, and re-layouts  1.31 us (6%)
  between operations  0.64 us (3%)
    pallas_call x1, Pallas kernels, on_device(): pl.pallas_call(functools.partial(kernel, sizes), out_shape=(pltpu.VMEM((l...  18.8 us
    unnamed x2, local copies, waits for them, and re-layouts  1.31 us

profile of v3, /device:TPU:0, one launch (start us, length us, event | category | flops | bytes accessed | tf_op | source)
XLA Modules:
  0.0 20.7 jit_solution(9041583393660660473)
XLA Ops:
  0.6 18.8 %shard_map.77 = (f32[2,64,512]{2,1,0:T(8,128)S(1)}, f32[2,16,128]{2,1,0:T(8,128)S(1)}) custom-call(bf16[4,2,64,512]{3,2,1,0:T(8,128)(2,1)} %inn_hbm.1, s32[2,2]{1,0:T(2,128)} %r_hbm.1, s32[2,2]{1,0:T(2,128)} %p_hbm.1, f32[2,16,128]{2,1,0:T(8,128)} %east.1, f32[2,16,128]{2,1,0:T(8,128)} %north.1, f32[2,16,128]{2,1,0:T(8,128)} %weight.1), custom_call_target="tpu_custom_call" | custom-call | tf_op jit(solution)/shard_map/pallas_call | solution.py:358
  19.4 0.7 %copy.10 = f32[2,64,512]{2,1,0:T(8,128)} copy(f32[2,64,512]{2,1,0:T(8,128)S(1)} %get-tuple-element.2) | data formatting | bytes 524288
  20.1 0.6 %copy.11 = f32[2,16,128]{2,1,0:T(8,128)} copy(f32[2,16,128]{2,1,0:T(8,128)S(1)} %get-tuple-element.3) | data formatting | bytes 32768

commit v4 on v3

--- a/solution.py
+++ b/solution.py
@@ -9,16 +9,16 @@
 
 MESH = pl.DeviceIdType.MESH
 HALO = 8
-SIDES = tuple((dx, dy) for dx in (0, 1, -1) for dy in (0, 1, -1) if dx or dy)
+SIDES = tuple((dx, dy) for dx in (1, -1, 0) for dy in (1, -1, 0) if dx or dy)
 F32, BF16 = jnp.float32, jnp.bfloat16
 
 
-def repeat(count, body):
-    if count <= 16:
-        for k in range(1, count):
+def repeat(offsets, body):
+    if len(offsets) <= 16:
+        for k in offsets:
             body(k)
     else:
-        lax.fori_loop(1, count, lambda k, carry: (body(k), carry)[1], 0)
+        lax.fori_loop(1, len(offsets) + 1, lambda k, carry: (body(k), carry)[1], 0)
 
 
 def split(values):
@@ -52,13 +52,19 @@
     ix, iy, il = lax.axis_index("gx"), lax.axis_index("gy"), lax.axis_index("lev")
     me = (ix * ny + iy) * nl + il
 
+    offsets = sorted(
+        range(1, group),
+        key=lambda k: (k % nl, k // (ny * nl) not in (0, 1, nx - 1), k // (ny * nl) == 0, k),
+    )
+
+    def peer_index(k):
+        return (
+            lax.rem(ix + k // (ny * nl), nx), lax.rem(iy + k // nl % ny, ny), lax.rem(il + k % nl, nl)
+        )
+
     def peer(k):
-        other = lax.rem(me + k, group)
-        return {
-            "gx": other // (ny * nl),
-            "gy": lax.rem(other // nl, ny),
-            "lev": lax.rem(other, nl),
-        }
+        x, y, l = peer_index(k)
+        return {"gx": x, "gy": y, "lev": l}
 
     loads = [
         pltpu.make_async_copy(src, dst, local.at[k])
@@ -75,7 +81,7 @@
     for ref in (c_rim, g_near, g_rim):
         ref[...] = jnp.zeros_like(ref)
     barrier = pltpu.get_barrier_semaphore()
-    repeat(group, lambda k: pl.semaphore_signal(barrier, inc=1, device_id=peer(k), device_id_type=MESH))
+    repeat(offsets, lambda k: pl.semaphore_signal(barrier, inc=1, device_id=peer(k), device_id_type=MESH))
     def wrapped(shape, dim):
         lane = iota(shape, dim)
         return jnp.where(lane < wide - wide // 4, lane, lane - wide)
@@ -262,30 +268,35 @@
     g = mine + jnp.concatenate([beside + unpack_all(near_rim), unpack_all(far_rim)], axis=1)
     g = jnp.where(inside, g, 0.0)
 
-    def hessian(p):
+    def sweep_ahead(p):
         states = []
-        state = p
         for _ in range(steps):
-            state = forward(state)
-            states.append(state)
-        lam = w_obs * states[-1]
+            p = forward(p)
+            states.append(p)
+        return states, [w_obs * state for state in states]
+
+    def sweep_back(weighted):
+        lam = weighted[-1]
         for t in range(steps - 2, -1, -1):
-            lam = adjoint(lam) + w_obs * states[t]
-        return p + adjoint(lam)
-
-    w = jnp.where(inside, hessian(g), 0.0)
-    v = hessian(w)
+            lam = adjoint(lam) + weighted[t]
+        return adjoint(lam)
 
     def own(x):
         return [x[l * ext + HALO : l * ext + HALO + rows, :cols] for l in range(levels)]
 
-    g_own, w_own, v_own = own(g), own(w), own(v)
+    w = jnp.where(inside, g + sweep_back(sweep_ahead(g)[1]), 0.0)
+    states, weighted = sweep_ahead(w)
+    g_own, w_own = own(g), own(w)
+    norms = [
+        sum((x * y for x, y in zip(xs, ys)), u * u)
+        for u, xs, ys in zip(w_own, zip(*map(own, states)), zip(*map(own, weighted)))
+    ]
 
     def partial(a, b):
         return sum(jnp.sum(x * y, axis=0, keepdims=True) for x, y in zip(a, b))
 
     gram = jnp.concatenate(
-        [partial(g_own, g_own), partial(g_own, w_own), partial(w_own, w_own), partial(w_own, v_own)]
+        [partial(g_own, g_own), partial(g_own, w_own), partial(w_own, w_own), partial(norms, [1.0] * levels)]
         + [jnp.zeros((4, cols), F32)], axis=0,
     )
     spread = jnp.sum(gram, axis=1, keepdims=True)
@@ -294,19 +305,20 @@
 
     def red_send(k):
         return pltpu.make_async_remote_copy(
-            src_ref=red.at[me], dst_ref=red.at[me], send_sem=r_send.at[k], recv_sem=r_recv.at[me],
+            src_ref=red.at[me], dst_ref=red.at[me], send_sem=r_send, recv_sem=r_recv,
             device_id=peer(k), device_id_type=MESH,
         )
 
-    def red_recv(k):
-        other = lax.rem(me + k, group)
-        return pltpu.make_async_remote_copy(
-            src_ref=red.at[me], dst_ref=red.at[other], send_sem=r_send.at[k],
-            recv_sem=r_recv.at[other], device_id=peer(k), device_id_type=MESH,
-        )
-
-    repeat(group, lambda k: red_send(k).start())
-
+    others = pl.ds(0, group - 1)
+    red_all = pltpu.make_async_remote_copy(
+        src_ref=red.at[others], dst_ref=red.at[others], send_sem=r_send, recv_sem=r_recv,
+        device_id=peer(1), device_id_type=MESH,
+    )
+
+    far_first = sorted(offsets, key=lambda k: (k // (ny * nl) in (0, 2), k // (ny * nl) == 0, -(k // nl % ny), k))
+    repeat(far_first, lambda k: red_send(k).start())
+
+    v_own = own(w + sweep_back(weighted))
     q_shape = (wide, fine_y)
     q_base = 0.25 * iota(q_shape, 1).astype(F32) - wrapped(q_shape, 0).astype(F32)
     b_shape = (fine_x, 2 * ext)
@@ -325,7 +337,7 @@
             dot(up, jnp.concatenate(split(across[k * ext : (k + 1) * ext]), axis=0)) for k in range(2)
         ])
 
-    repeat(group, lambda k: red_recv(k).wait_recv())
+    red_all.wait_recv()
     sums = jnp.sum(red[...], axis=0)
     gg, gw, ww, wv = (sums[:, k * (cols // 4)][:, None] for k in range(4))
     alpha = gg / gw
@@ -344,7 +356,18 @@
 
     wait_send_all(coef_copies)
     wait_send_all(g_copies)
-    repeat(group, lambda k: red_send(k).wait_send())
+    red_all.wait_send()
+
+
+def store(increment, residual, out, res, sems):
+    copies = [
+        pltpu.make_async_copy(src, dst, sems.at[k])
+        for k, (src, dst) in enumerate([(increment, out), (residual, res)])
+    ]
+    for copy in copies:
+        copy.start()
+    for copy in copies:
+        copy.wait()
 
 
 def on_device(sizes, innovations, restrict_offsets, prolong_offsets, east, north, weight):
@@ -355,7 +378,7 @@
     vmem = pl.BlockSpec(memory_space=pltpu.VMEM)
     hbm = pl.BlockSpec(memory_space=pltpu.HBM)
     dma = pltpu.SemaphoreType.DMA
-    return pl.pallas_call(
+    made = pl.pallas_call(
         functools.partial(kernel, sizes),
         out_shape=(
             pltpu.VMEM((levels, fine_x, fine_y), F32),
@@ -375,12 +398,19 @@
             pltpu.VMEM((3, HALO, cols), F32),
             pltpu.VMEM((levels, ext, cols), F32),
             pltpu.VMEM((group, 1, cols), F32),
-            dma((6,)), dma((8,)), dma((8,)), dma((16,)), dma((16,)), dma((group,)), dma((group,)),
+            dma((6,)), dma((8,)), dma((8,)), dma((16,)), dma((16,)), dma, dma,
         ],
         compiler_params=pltpu.CompilerParams(
             collective_id=0, has_side_effects=True
         ),
     )(innovations, restrict_offsets, prolong_offsets, east, north, weight)
+    return pl.pallas_call(
+        store,
+        out_shape=tuple(jax.ShapeDtypeStruct(x.shape, F32) for x in made),
+        in_specs=[vmem, vmem],
+        out_specs=(hbm, hbm),
+        scratch_shapes=[dma((2,))],
+    )(*(pltpu.with_memory_space_constraint(x, pltpu.VMEM) for x in made))
 
 
 def solution(mesh):

time: 20.9 us -> 19.4 us (0.928)
  local copies, waits for them, and re-layouts: 1.31 us -> 0 us
    unnamed x2 -> x0, local copies, waits for them, and re-layouts: 1.31 us -> none
    pallas_call x1, Pallas kernels: 18.8 us -> 17.9 us  [on_device(): pl.pallas_call(functools.partial(kernel, sizes), out_shape=(pltpu.VMEM((l...]
    pallas_call x0 -> x1, Pallas kernels: none -> 0.72 us  [on_device(): pl.pallas_call(store, out_shape=tuple((jax.ShapeDtypeStruct(x.shape, F32)...]
where the time goes in v4:
time: 19.4 us; the launch traced here: 19.3 us
  Pallas kernels  18.6 us (96%)
  between operations  0.64 us (3%)
    pallas_call x1, Pallas kernels, on_device(): pl.pallas_call(functools.partial(kernel, sizes), out_shape=(pltpu.VMEM((l...  17.9 us
    pallas_call x1, Pallas kernels, on_device(): pl.pallas_call(store, out_shape=tuple((jax.ShapeDtypeStruct(x.shape, F32)...  0.72 us

profile of v4, /device:TPU:0, one launch (start us, length us, event | category | flops | bytes accessed | tf_op | source)
XLA Modules:
  0.0 19.3 jit_solution(5040937084096524194)
XLA Ops:
  0.6 17.9 %shard_map.77 = (f32[2,64,512]{2,1,0:T(8,128)S(1)}, f32[2,16,128]{2,1,0:T(8,128)S(1)}) custom-call(bf16[4,2,64,512]{3,2,1,0:T(8,128)(2,1)} %inn_hbm.1, s32[2,2]{1,0:T(2,128)} %r_hbm.1, s32[2,2]{1,0:T(2,128)} %p_hbm.1, f32[2,16,128]{2,1,0:T(8,128)} %east.1, f32[2,16,128]{2,1,0:T(8,128)} %north.1, f32[2,16,128]{2,1,0:T(8,128)} %weight.1), custom_call_target="tpu_custom_call" | custom-call | tf_op jit(solution)/shard_map/pallas_call | solution.py:381
  18.5 0.7 %shard_map.78 = (f32[2,64,512]{2,1,0:T(8,128)}, f32[2,16,128]{2,1,0:T(8,128)}) custom-call(f32[2,64,512]{2,1,0:T(8,128)S(1)} %get-tuple-element.4.increment, f32[2,16,128]{2,1,0:T(8,128)S(1)} %get-tuple-element.5.residual), custom_call_target="tpu_custom_call" | custom-call | tf_op jit(solution)/shard_map/pallas_call | solution.py:407

commit v5 on v4

--- a/solution.py
+++ b/solution.py
@@ -80,34 +80,31 @@
     coef[:, :, HALO + rows :] = edge
     for ref in (c_rim, g_near, g_rim):
         ref[...] = jnp.zeros_like(ref)
-    barrier = pltpu.get_barrier_semaphore()
-    repeat(offsets, lambda k: pl.semaphore_signal(barrier, inc=1, device_id=peer(k), device_id_type=MESH))
-    def wrapped(shape, dim):
-        lane = iota(shape, dim)
-        return jnp.where(lane < wide - wide // 4, lane, lane - wide)
-
-    a_shape = (steps * ext, steps * fine_x)
-    a_row, a_col = iota(a_shape, 0), iota(a_shape, 1)
-    a_same = a_row // ext == a_col // fine_x
-    a_base = 0.25 * (a_col % fine_x - 4 * (a_row % ext - HALO)).astype(F32)
-    a_base = jnp.where(a_same, a_base, 1e6)
-    c_shape = (fine_y, wide)
-    c_base = 0.25 * (iota(c_shape, 0) - 4 * wrapped(c_shape, 1)).astype(F32)
-
-    def tent(base, offset):
-        return jnp.maximum(0.5 - jnp.abs(base - (offset.astype(F32) + 0.5) * 0.25), 0.0).astype(BF16)
-
-    loads[3].wait()
-    a_mats = [tent(a_base, r_off[level, 0]) for level in range(levels)]
-    c_mats = [tent(c_base, r_off[level, 1]) for level in range(levels)]
-
-    pl.semaphore_wait(barrier, group - 1)
-    for load in loads[:3]:
-        load.wait()
-
     def present(dx, dy):
         x, y = ix + dx, iy + dy
         return (x >= 0) & (x < nx) & (y >= 0) & (y < ny)
+
+    barrier = pltpu.get_barrier_semaphore()
+    if nx <= 4 and ny <= 2 and nl == 2:
+        greeted = [(dx, dy, 0) for dx, dy in sorted(SIDES, key=lambda side: abs(side[0]) + abs(side[1]))]
+        greeted += [(1, 0, 1), (-1, 0, 1)]
+        count = 1
+        for dx, dy, other in greeted:
+            here = present(dx, dy)
+            count += here.astype(jnp.int32)
+
+            @pl.when(here)
+            def _():
+                target = {"gx": ix + dx, "gy": iy + dy, "lev": 1 - il if other else il}
+                pl.semaphore_signal(barrier, inc=1, device_id=target, device_id_type=MESH)
+
+        pl.semaphore_signal(barrier, inc=1, device_id={"lev": 1 - il}, device_id_type=MESH)
+        pl.semaphore_wait(barrier, count)
+    else:
+        repeat(offsets, lambda k: pl.semaphore_signal(barrier, inc=1, device_id=peer(k), device_id_type=MESH))
+        pl.semaphore_wait(barrier, group - 1)
+    for load in loads[:3]:
+        load.wait()
 
     def remote(src, dst, send, recv, dx, dy):
         return pltpu.make_async_remote_copy(
@@ -191,6 +188,26 @@
         return SIDES.index((-dx, -dy))
 
     start_all(coef_copies)
+
+    def wrapped(shape, dim):
+        lane = iota(shape, dim)
+        return jnp.where(lane < wide - wide // 4, lane, lane - wide)
+
+    a_shape = (steps * ext, steps * fine_x)
+    a_row, a_col = iota(a_shape, 0), iota(a_shape, 1)
+    a_same = a_row // ext == a_col // fine_x
+    a_base = 0.25 * (a_col % fine_x - 4 * (a_row % ext - HALO)).astype(F32)
+    a_base = jnp.where(a_same, a_base, 1e6)
+    c_shape = (fine_y, wide)
+    c_base = 0.25 * (iota(c_shape, 0) - 4 * wrapped(c_shape, 1)).astype(F32)
+
+    def tent(base, offset):
+        return jnp.maximum(0.5 - jnp.abs(base - (offset.astype(F32) + 0.5) * 0.25), 0.0).astype(BF16)
+
+    loads[3].wait()
+    a_mats = [tent(a_base, r_off[level, 0]) for level in range(levels)]
+    c_mats = [tent(c_base, r_off[level, 1]) for level in range(levels)]
+
 
     loads[4].wait()
     restricted = []

time: 19.4 us -> 18.6 us (0.959)
  Pallas kernels: 18.6 us -> 17.8 us
    pallas_call x1, Pallas kernels: 17.9 us -> 17.1 us  [on_device(): pl.pallas_call(functools.partial(kernel, sizes), out_shape=(pltpu.VMEM((l...]
where the time goes in v5:
time: 18.6 us; the launch traced here: 18.5 us
  Pallas kernels  17.8 us (96%)
  between operations  0.64 us (3%)
    pallas_call x1, Pallas kernels, on_device(): pl.pallas_call(functools.partial(kernel, sizes), out_shape=(pltpu.VMEM((l...  17.1 us
    pallas_call x1, Pallas kernels, on_device(): pl.pallas_call(store, out_shape=tuple((jax.ShapeDtypeStruct(x.shape, F32)...  0.72 us

profile of v5, /device:TPU:0, one launch (start us, length us, event | category | flops | bytes accessed | tf_op | source)
XLA Modules:
  0.0 18.5 jit_solution(12996202967325209512)
XLA Ops:
  0.6 17.1 %shard_map.77 = (f32[2,64,512]{2,1,0:T(8,128)S(1)}, f32[2,16,128]{2,1,0:T(8,128)S(1)}) custom-call(bf16[4,2,64,512]{3,2,1,0:T(8,128)(2,1)} %inn_hbm.1, s32[2,2]{1,0:T(2,128)} %r_hbm.1, s32[2,2]{1,0:T(2,128)} %p_hbm.1, f32[2,16,128]{2,1,0:T(8,128)} %east.1, f32[2,16,128]{2,1,0:T(8,128)} %north.1, f32[2,16,128]{2,1,0:T(8,128)} %weight.1), custom_call_target="tpu_custom_call" | custom-call | tf_op jit(solution)/shard_map/pallas_call | solution.py:398
  17.7 0.7 %shard_map.78 = (f32[2,64,512]{2,1,0:T(8,128)}, f32[2,16,128]{2,1,0:T(8,128)}) custom-call(f32[2,64,512]{2,1,0:T(8,128)S(1)} %get-tuple-element.4.increment, f32[2,16,128]{2,1,0:T(8,128)S(1)} %get-tuple-element.5.residual), custom_call_target="tpu_custom_call" | custom-call | tf_op jit(solution)/shard_map/pallas_call | solution.py:424

commit v6 on v5

--- a/solution.py
+++ b/solution.py
@@ -114,7 +114,7 @@
 
     half = ext // 2
     coef_rows = {1: (rows, 0), -1: (HALO, HALO + rows)}
-    half_rows = {1: (half, 0), -1: (0, half)}
+    half_end = levels * half
 
     def coef_copies(number, dx, dy):
         sems = c_send.at[number], c_recv.at[number]
@@ -124,16 +124,11 @@
         return [remote(coef.at[:, :, pl.ds(src, HALO)], coef.at[:, :, pl.ds(dst, HALO)], *sems, dx, dy)]
 
     def g_copies(number, dx, dy):
-        slot = {1: 0, -1: 1, 0: 2}[dy]
-        found = [remote(g_pack.at[slot], g_rim.at[number], g_send.at[number], g_recv.at[number], dx, dy)]
-        if dy == 0:
-            src, dst = half_rows[dx]
-            extra = len(SIDES) + number
-            found.append(remote(
-                near_out.at[:, pl.ds(src, half)], g_near.at[:, pl.ds(dst, half)],
-                g_send.at[extra], g_recv.at[extra], dx, dy,
-            ))
-        return found
+        sems = g_send.at[number], g_recv.at[number]
+        if dy:
+            return [remote(g_pack.at[0 if dy == 1 else 1], g_rim.at[number], *sems, dx, dy)]
+        src, dst = (1, 0) if dx == 1 else (0, 1)
+        return [remote(near_out.at[src], g_near.at[dst], *sems, dx, dy)]
 
     def start_all(make):
         for number, (dx, dy) in enumerate(SIDES):
@@ -242,12 +237,13 @@
     def forward(x):
         return stay * x + e * pltpu.roll(x, 1, 0) + n * pltpu.roll(x, 1, 1)
 
-    def adjoint(y):
-        return stay * y + pltpu.roll(e * y, total_rows - 1, 0) + pltpu.roll(n * y, wide - 1, 1)
+    def adjoint(y, added=None):
+        here = stay * y if added is None else stay * y + added
+        return here + pltpu.roll(e * y, total_rows - 1, 0) + pltpu.roll(n * y, wide - 1, 1)
 
     lam = w_obs * at_time(steps - 1)
     for t in range(steps - 2, -1, -1):
-        lam = adjoint(lam) + w_obs * at_time(t)
+        lam = adjoint(lam, w_obs * at_time(t))
     mine = adjoint(lam)
     near, far = mine[:, :cols], mine[:, cols:]
     tiles = total_rows // HALO
@@ -255,8 +251,11 @@
     far_pack = pack([far[HALO * k : HALO * (k + 1)] for k in range(tiles)])
     g_pack[0] = jnp.where(upper, near_pack, far_pack)
     g_pack[1] = jnp.where(upper, far_pack, near_pack)
-    g_pack[2] = far_pack
-    near_out[...] = near.reshape(levels, ext, cols)
+    for side in range(2):
+        for level in range(levels):
+            start = level * ext + side * half
+            near_out[side, level * half : (level + 1) * half] = near[start : start + half]
+        near_out[side, half_end:] = far_pack
     start_all(g_copies)
 
     m_shape = (total_rows, wide)
@@ -269,8 +268,11 @@
     first_half = window % ext_tiles < ext_tiles // 2
 
     def shifted(dy):
-        back = turn(g_rim[arrived(-1, dy)], -(ext_tiles // 2))
-        ahead = turn(g_rim[arrived(1, dy)], ext_tiles // 2)
+        if dy:
+            back, ahead = g_rim[arrived(-1, dy)], g_rim[arrived(1, dy)]
+        else:
+            back, ahead = g_near[0, half_end:], g_near[1, half_end:]
+        back, ahead = turn(back, -(ext_tiles // 2)), turn(ahead, ext_tiles // 2)
         return jnp.where(first_half, back, ahead)
 
     from_left = g_rim[arrived(0, -1)] + shifted(-1)
@@ -281,7 +283,10 @@
     def unpack_all(packed):
         return jnp.concatenate([unpack(packed, k) for k in range(tiles)], axis=0)
 
-    beside = g_near[...].reshape(total_rows, cols)
+    beside = jnp.concatenate([
+        g_near[side, level * half : (level + 1) * half]
+        for level in range(levels) for side in range(2)
+    ], axis=0)
     g = mine + jnp.concatenate([beside + unpack_all(near_rim), unpack_all(far_rim)], axis=1)
     g = jnp.where(inside, g, 0.0)
 
@@ -292,16 +297,16 @@
             states.append(p)
         return states, [w_obs * state for state in states]
 
-    def sweep_back(weighted):
+    def sweep_back(weighted, added):
         lam = weighted[-1]
         for t in range(steps - 2, -1, -1):
-            lam = adjoint(lam) + weighted[t]
-        return adjoint(lam)
+            lam = adjoint(lam, weighted[t])
+        return adjoint(lam, added)
 
     def own(x):
         return [x[l * ext + HALO : l * ext + HALO + rows, :cols] for l in range(levels)]
 
-    w = jnp.where(inside, g + sweep_back(sweep_ahead(g)[1]), 0.0)
+    w = jnp.where(inside, sweep_back(sweep_ahead(g)[1], g), 0.0)
     states, weighted = sweep_ahead(w)
     g_own, w_own = own(g), own(w)
     norms = [
@@ -335,7 +340,7 @@
     far_first = sorted(offsets, key=lambda k: (k // (ny * nl) in (0, 2), k // (ny * nl) == 0, -(k // nl % ny), k))
     repeat(far_first, lambda k: red_send(k).start())
 
-    v_own = own(w + sweep_back(weighted))
+    v_own = own(sweep_back(weighted, w))
     q_shape = (wide, fine_y)
     q_base = 0.25 * iota(q_shape, 1).astype(F32) - wrapped(q_shape, 0).astype(F32)
     b_shape = (fine_x, 2 * ext)
@@ -410,12 +415,12 @@
             pltpu.VMEM((3, levels, ext, cols), F32),
             pltpu.VMEM((8, 2, HALO, cols), F32),
             pltpu.VMEM((2, HALO, cols), F32),
-            pltpu.VMEM((levels, ext, cols), F32),
+            pltpu.VMEM((2, levels * ext // 2 + HALO, cols), F32),
             pltpu.VMEM((8, HALO, cols), F32),
-            pltpu.VMEM((3, HALO, cols), F32),
-            pltpu.VMEM((levels, ext, cols), F32),
+            pltpu.VMEM((2, HALO, cols), F32),
+            pltpu.VMEM((2, levels * ext // 2 + HALO, cols), F32),
             pltpu.VMEM((group, 1, cols), F32),
-            dma((6,)), dma((8,)), dma((8,)), dma((16,)), dma((16,)), dma, dma,
+            dma((6,)), dma((8,)), dma((8,)), dma((8,)), dma((8,)), dma, dma,
         ],
         compiler_params=pltpu.CompilerParams(
             collective_id=0, has_side_effects=True

time: 18.6 us -> 18.5 us (level)
  no operation moved by 1% of the time
where the time goes in v6:
time: 18.5 us; the launch traced here: 18.3 us
  Pallas kernels  17.7 us (96%)
  between operations  0.64 us (3%)
    pallas_call x1, Pallas kernels, on_device(): pl.pallas_call(functools.partial(kernel, sizes), out_shape=(pltpu.VMEM((l...  17 us
    pallas_call x1, Pallas kernels, on_device(): pl.pallas_call(store, out_shape=tuple((jax.ShapeDtypeStruct(x.shape, F32)...  0.72 us

profile of v6, /device:TPU:0, one launch (start us, length us, event | category | flops | bytes accessed | tf_op | source)
XLA Modules:
  0.0 18.3 jit_solution(2622643733095912069)
XLA Ops:
  0.6 17.0 %shard_map.77 = (f32[2,64,512]{2,1,0:T(8,128)S(1)}, f32[2,16,128]{2,1,0:T(8,128)S(1)}) custom-call(bf16[4,2,64,512]{3,2,1,0:T(8,128)(2,1)} %inn_hbm.1, s32[2,2]{1,0:T(2,128)} %r_hbm.1, s32[2,2]{1,0:T(2,128)} %p_hbm.1, f32[2,16,128]{2,1,0:T(8,128)} %east.1, f32[2,16,128]{2,1,0:T(8,128)} %north.1, f32[2,16,128]{2,1,0:T(8,128)} %weight.1), custom_call_target="tpu_custom_call" | custom-call | tf_op jit(solution)/shard_map/pallas_call | solution.py:403
  17.6 0.7 %shard_map.78 = (f32[2,64,512]{2,1,0:T(8,128)}, f32[2,16,128]{2,1,0:T(8,128)}) custom-call(f32[2,64,512]{2,1,0:T(8,128)S(1)} %get-tuple-element.4.increment, f32[2,16,128]{2,1,0:T(8,128)S(1)} %get-tuple-element.5.residual), custom_call_target="tpu_custom_call" | custom-call | tf_op jit(solution)/shard_map/pallas_call | solution.py:429
